TPU v7x, 1024 devices: a whole 4x4x32 slice. The times are simulated.
1024 devices in a mesh: dp: 64 (over z, core), expert: 16 (over y, x).
Axes of the slice: x: 4, y: 4, z: 32, core: 2. Of those that a mesh axis runs over, the one named last changes fastest.
Arguments:
- tokens: bfloat16 [512, 3072], P('dp', 'expert'), may hold values from -6 to 6
- grad_out: bfloat16 [512, 3072], P('dp', 'expert'), may hold values from -1.5 to 1.5
- routes: int32 [512, 4], P('dp'), may hold values from 0 to 15, all different within a row; in each aligned block of 8 rows (0 to 7, 8 to 15, ...) at most 4 rows name the same one
- gate_probs: float32 [512, 4], P('dp'), may hold values from 0.1 to 1
- w_gate: bfloat16 [16, 6144, 3072], P('expert', 'dp'), may hold values from -0.109375 to 0.109375
- w_up: bfloat16 [16, 6144, 3072], P('expert', 'dp'), may hold values from -0.109375 to 0.109375
- w_down: bfloat16 [16, 6144, 3072], P('expert', 'dp'), may hold values from -0.078125 to 0.078125
Outputs:
- grad_in: bfloat16 [512, 3072], P('dp', 'expert')
- grad_gate: bfloat16 [16, 6144, 3072], P('expert', 'dp')
- grad_up: bfloat16 [16, 6144, 3072], P('expert', 'dp')
- grad_down: bfloat16 [16, 6144, 3072], P('expert', 'dp')
Inputs may be any that keep to these rules, and one draw needn't show every extreme that they name: `routes`: each token names 4 different experts. Among the 8 tokens of one dp index no expert is named more than 4 times, and in every draw some expert is named exactly 4 times by the tokens of some dp index.
All inputs are finite; a program needn't handle non-finite values.
Results may differ from a plain program's by a relative error of at most 0.0064.
Values may be sent and summed in bfloat16 or wider, within the bound.
No kernel may reach another device: no remote copies, remote signals or barrier semaphores. Data moves between devices by JAX's collectives and lax.ppermute only.
A program may use at most 32 MiB of HBM per device.

v0:
```python
import jax
import jax.numpy as jnp
from jax import lax
from jax.sharding import PartitionSpec as P

EXPERTS = 16
CAP = 4


def silu_parts(pre_act):
    sigmoid_val = jax.nn.sigmoid(pre_act)
    return (pre_act * sigmoid_val, sigmoid_val * (1.0 + pre_act * (1.0 - sigmoid_val)))


def slot_tables(route_rows, prob_rows, experts, capacity):
    tok_rows, top_k = route_rows.shape
    flat_routes = route_rows.reshape(tok_rows * top_k)
    onehot = (flat_routes[:, None] == jnp.arange(experts, dtype=jnp.int32)[None, :]).astype(
        jnp.int32
    )
    before = jnp.cumsum(onehot, axis=0) - onehot
    slot_index = jnp.sum(onehot * before, axis=1)
    slot_place = slot_index * experts + flat_routes
    placement = (
        slot_place[:, None] == jnp.arange(capacity * experts, dtype=jnp.int32)[None, :]
    ).astype(prob_rows.dtype)
    placement = placement.reshape(tok_rows, top_k, capacity * experts)
    dispatch = jnp.sum(placement, axis=1)
    weighted = jnp.sum(placement * prob_rows[:, :, None], axis=1)
    return (dispatch, weighted)


def shards(tokens, grad_out, routes, gate_probs, w_gate, w_up, w_down):
    tok_rows, slice_width = tokens.shape
    dispatch, weighted = slot_tables(routes, gate_probs, EXPERTS, CAP)
    rows_first = (((0,), (0,)), ((), ()))
    packed_in = lax.dot_general(
        dispatch.astype(jnp.bfloat16), tokens, rows_first, preferred_element_type=jnp.float32
    ).astype(jnp.bfloat16)
    packed_grad = lax.dot_general(
        weighted,
        grad_out.astype(jnp.float32),
        rows_first,
        precision=lax.Precision.HIGHEST,
        preferred_element_type=jnp.float32,
    ).astype(jnp.bfloat16)
    packed_in = packed_in.reshape(CAP, EXPERTS, slice_width)
    packed_grad = packed_grad.reshape(CAP, EXPERTS, slice_width)
    mine_in, mine_grad = (
        lax.all_to_all(packed_in, "expert", split_axis=1, concat_axis=2, tiled=True),
        lax.all_to_all(packed_grad, "expert", split_axis=1, concat_axis=2, tiled=True),
    )
    rows_in, rows_grad = (
        lax.all_gather(mine_in, "dp", axis=0, tiled=True),
        lax.all_gather(mine_grad, "dp", axis=0, tiled=True),
    )
    pre_act = jnp.einsum("jfd,rjd->jfr", w_gate, rows_in, preferred_element_type=jnp.float32)
    up_value = jnp.einsum("jfd,rjd->jfr", w_up, rows_in, preferred_element_type=jnp.float32)
    silu_val, silu_slope = silu_parts(pre_act)
    activation = (silu_val * up_value).astype(jnp.bfloat16)
    grad_act = jnp.einsum("jfd,rjd->jfr", w_down, rows_grad, preferred_element_type=jnp.float32)
    grad_pre = (grad_act * up_value * silu_slope).astype(jnp.bfloat16)
    grad_upv = (grad_act * silu_val).astype(jnp.bfloat16)
    total = jnp.einsum("jfr,jfd->rjd", grad_pre, w_gate, preferred_element_type=jnp.float32)
    back_rows = lax.psum_scatter(
        total + jnp.einsum("jfr,jfd->rjd", grad_upv, w_up, preferred_element_type=jnp.float32),
        "dp",
        scatter_dimension=0,
        tiled=True,
    ).astype(jnp.bfloat16)
    grad_gate = jnp.einsum("jfr,rjd->jfd", grad_pre, rows_in, preferred_element_type=jnp.float32)
    grad_up = jnp.einsum("jfr,rjd->jfd", grad_upv, rows_in, preferred_element_type=jnp.float32)
    grad_down = jnp.einsum(
        "jfr,rjd->jfd", activation, rows_grad, preferred_element_type=jnp.float32
    )
    grad_gate, grad_up, grad_down = (
        grad_gate.astype(jnp.bfloat16),
        grad_up.astype(jnp.bfloat16),
        grad_down.astype(jnp.bfloat16),
    )
    returned = lax.all_to_all(back_rows, "expert", split_axis=2, concat_axis=1, tiled=True)
    returned = returned.reshape(CAP * EXPERTS, slice_width)
    grad_in = jnp.dot(
        dispatch.astype(jnp.bfloat16), returned, preferred_element_type=jnp.float32
    ).astype(jnp.bfloat16)
    return (grad_in, grad_gate, grad_up, grad_down)


def solution(mesh):
    in_specs = (
        P("dp", "expert"),
        P("dp", "expert"),
        P("dp", None),
        P("dp", None),
        P("expert", "dp", None),
        P("expert", "dp", None),
        P("expert", "dp", None),
    )
    out_specs = (
        P("dp", "expert"),
        P("expert", "dp", None),
        P("expert", "dp", None),
        P("expert", "dp", None),
    )
    return jax.shard_map(shards, mesh=mesh, in_specs=in_specs, out_specs=out_specs, check_vma=False)
```

profile of v0, /device:TPU:1, one launch (start us, length us, event | category | flops | bytes accessed | tf_op | source)
XLA Modules:
  0.0 566.1 jit_solution(2343574884988488290)
XLA Ops:
  7.2 0.8 copy.34
  8.6 0.8 select_reduce_fusion
  9.4 0.9 convolution_convert_fusion.3
  10.3 13.8 %all_to_all.35 = bf16[4,16,192]{2,0,1:T(4,128)(2,1)S(1)} all-to-all(bf16[4,16,192]{2,0,1:T(4,128)(2,1)S(1)} %copy.40), channel_id=1, replica_groups=mesh['dp'=64,'expert'=16] {'expert'}, dimensions={1} | all-to-all | bytes 49152 | tf_op jit(solution)/shard_map/all_to_all | solution.py:50
  25.0 0.9 convolution_convert_fusion.4
  25.9 9.2 %all_to_all.36 = bf16[4,16,192]{2,0,1:T(4,128)(2,1)S(1)} all-to-all(bf16[4,16,192]{2,0,1:T(4,128)(2,1)S(1)} %copy.37), channel_id=1, replica_groups=mesh['dp'=64,'expert'=16] {'expert'}, dimensions={1} | all-to-all | bytes 49152 | tf_op jit(solution)/shard_map/all_to_all | solution.py:51
  35.9 1.3 dynamic-slice
  37.8 131.1 %all-gather.5.cloned.1.call-done = bf16[256,1,3072]{2,1,0:T(2,128)(2,1)} async-done(((bf16[4,1,3072]{2,1,0:T(2,128)(2,1)}), bf16[256,1,3072]{2,1,0:T(2,128)(2,1)}) %all-gather.5.cloned.1.call-update) | async-done | bytes 1572880 | tf_op jit(solution)/shard_map/all_gather | solution.py:54
  168.9 2.4 copy.48
  173.0 128.5 %all-gather.3.cloned.1.call-done = bf16[256,1,3072]{2,1,0:T(2,128)(2,1)} async-done(((bf16[4,1,3072]{2,1,0:T(2,128)(2,1)}), bf16[256,1,3072]{2,1,0:T(2,128)(2,1)}) %all-gather.3.cloned.1.call-update) | async-done | bytes 1572880 | tf_op jit(solution)/shard_map/all_gather | solution.py:55
  301.5 2.7 multiply_convert_fusion.1
  304.2 1.2 fusion.2
  306.0 2.3 fusion
  308.3 209.6 %all-reduce.2 = bf16[256,1,3072]{2,0,1:T(8,128)(2,1)} all-reduce(f32[256,1,3072]{2,0,1:T(8,128)} %fusion), channel_id=2, replica_groups=mesh['dp'=64,'expert'=16] {'dp'}, use_global_device_ids=true, to_apply=%region_4.5.clone | all-reduce | flops 786432 | bytes 4718592
  517.8 0.8 dynamic-slice_convert_fusion
  518.6 3.0 copy.43
  522.1 18.0 %reduce = bf16[3072,4]{1,0:T(8,128)(2,1)S(1)} reduce(bf16[3072,1,4]{2,1,0:T(2,128)(2,1)} %bitcast.72, bf16[]{:T(256)} %broadcast.37), dimensions={1}, to_apply=%bitcast.56.reduce_sub_computation | reduce | bytes 49154
  540.1 2.0 reshape.119
  542.1 6.6 %all-to-all-start.2 = ((bf16[16,2,384]{2,1,0:T(2,128)(2,1)}), bf16[16,2,384]{2,1,0:T(2,128)(2,1)S(1)}, u32[]{:S(2)}, u32[]{:S(2)}) async-start(bf16[16,2,384]{2,1,0:T(2,128)(2,1)} %reshape.119), calls=%async_computation.2 | async-start | bytes 49152 | tf_op jit(solution)/shard_map/all_to_all | solution.py:81
  548.7 3.4 fusion.3
  552.0 1.2 fusion.1
  553.2 1.9 all-to-all-done.2
  555.1 2.0 reshape.120
  557.1 1.3 copy.44
  (28 shorter events, 5.8 us)
Async XLA Ops:
  7.2 164.1 %copy-start = (bf16[1,96,3072]{2,1,0:T(8,128)(2,1)S(1)}, bf16[1,96,3072]{2,1,0:T(8,128)(2,1)}, u32[]{:S(2)}) copy-start(bf16[1,96,3072]{2,1,0:T(8,128)(2,1)} %param.11) | copy-start | bytes 1769476
  7.2 161.8 %all-gather.5.cloned.1.call-start = ((), (), s32[]{:S(2)}) async-start(), calls=%async_computation.4 | async-start | bytes 3194880 | tf_op jit(solution)/shard_map/all_gather | solution.py:54
  24.9 276.6 %all-gather.3.cloned.1.call-start = ((), (), s32[]{:S(2)}) async-start(), calls=%async_computation.3 | async-start | bytes 3194880 | tf_op jit(solution)/shard_map/all_gather | solution.py:55
  171.3 1.1 copy-start.1
  542.1 13.0 %all-to-all-start.2 = ((bf16[16,2,384]{2,1,0:T(2,128)(2,1)}), bf16[16,2,384]{2,1,0:T(2,128)(2,1)S(1)}, u32[]{:S(2)}, u32[]{:S(2)}) async-start(bf16[16,2,384]{2,1,0:T(2,128)(2,1)} %reshape.119), calls=%async_computation.2 | async-start | bytes 49152 | tf_op jit(solution)/shard_map/all_to_all | solution.py:81
Sparse Core Ops, SparseCore 0:
  25.0 143.8 all-gather.4
  172.2 129.2 all-gather.2
where the time goes:
time: 570 us; the launch traced here: 566 us
  waiting for transfers between devices  261 us (46%)
  blocking collectives  233 us (41%)
  other arithmetic  19.1 us (3%)
  local copies, waits for them, and re-layouts  16.3 us (3%)
  matrix products  15.1 us (3%)
  between operations  14.8 us (3%)
  starting transfers between devices  6.64 us (1%)
    unnamed x1, blocking collectives  210 us
    all_gather x1, waiting for transfers between devices, shards(): lax.all_gather(mine_in, 'dp', axis=0, tiled=True)  131 us
    all_gather x1, waiting for transfers between devices, shards(): lax.all_gather(mine_grad, 'dp', axis=0, tiled=True)  128 us
    unnamed x1, other arithmetic  18 us
    all_to_all x1, blocking collectives, shards(): lax.all_to_all(packed_in, 'expert', split_axis=1, concat_axis=2, tiled=True)  13.8 us
  transfers between devices with their start and end apart: 3, of which 3 were waited for; matrix products, arithmetic and copies ran while one was open for 2% of the time, Pallas kernels for 0%

commit v1 on v0

v1 whole, which is shorter than its diff:
```python
import jax
import jax.numpy as jnp
from jax import lax
from jax.experimental import pallas as pl
from jax.experimental.pallas import tpu as pltpu
from jax.sharding import Mesh, PartitionSpec as P

EXPERTS = 16
CAP = 4
TOP = 4
FAR = 8
NEAR = 4
BF16 = jnp.bfloat16
F32 = jnp.float32
VMEM_BYTES = 48 * 1024 * 1024
GRAD_AT = 256
ROW = 512


def message_kernel(tokens_ref, grad_ref, routes_ref, probs_ref, out_ref):
    tok_rows, width = tokens_ref.shape
    routes = routes_ref[...].astype(F32)
    probs = probs_ref[...]
    lane = lax.broadcasted_iota(jnp.int32, (tok_rows, 128), 1)
    row = lax.broadcasted_iota(jnp.int32, (tok_rows, 128), 0)
    lane_f = lane.astype(F32)
    onehot = jnp.zeros((tok_rows, 128), F32)
    for k in range(TOP):
        onehot = jnp.where(lane_f == routes[:, k : k + 1], 1.0, onehot)
    before = jnp.zeros((tok_rows, 128), F32)
    for s in range(1, tok_rows):
        before = before + jnp.where(row >= s, pltpu.roll(onehot, s, 0), 0.0)
    meta = jnp.zeros((tok_rows, 128), F32)
    base = width - 128
    for k in range(TOP):
        chosen = routes[:, k : k + 1]
        slot = jnp.sum(jnp.where(lane_f == chosen, before, 0.0), axis=1, keepdims=True)
        meta = jnp.where(lane == base + k, chosen * CAP + slot, meta)
        rest = probs[:, k : k + 1]
        for part in range(3):
            piece = rest.astype(BF16).astype(F32)
            meta = jnp.where(lane == base + (part + 1) * TOP + k, piece, meta)
            rest = rest - piece
    meta = meta.astype(BF16)
    tail = jnp.zeros((tok_rows, 128), BF16)
    for copy in range(out_ref.shape[0]):
        out_ref[copy, :, 128:256] = meta
        out_ref[copy, :, 0:width] = tokens_ref[...]
        out_ref[copy, :, GRAD_AT + 128 : GRAD_AT + 256] = tail
        out_ref[copy, :, GRAD_AT : GRAD_AT + width] = grad_ref[...]


def message(tokens, grad_out, routes, probs):
    return pl.pallas_call(
        message_kernel,
        out_shape=jax.ShapeDtypeStruct((FAR, tokens.shape[0], ROW), BF16),
    )(tokens, grad_out, routes, probs)


def pack_kernel(msg_ref, out_ref, place_ref, diff_ref):
    toks = msg_ref.shape[0]
    width = out_ref.shape[1]
    rows = out_ref.shape[2] // 2
    left = msg_ref[:, 0:256].astype(F32)
    feats = jnp.transpose(left).astype(BF16)[:width]
    cots = jnp.transpose(msg_ref[:, GRAD_AT : GRAD_AT + 256].astype(F32)).astype(BF16)[:width]
    tok = lax.broadcasted_iota(jnp.int32, (toks, rows), 0)
    row = lax.broadcasted_iota(jnp.int32, (toks, rows), 1)
    same = (tok >> 3) == (row >> 2)
    slot = (row & 3).astype(F32)
    weights = []
    for k in range(TOP):
        code = left[:, width + k : width + k + 1]
        diff_ref[k] = jnp.where(same, code - slot, -1.0)
        at = width + TOP + k
        weights.append(
            left[:, at : at + 1] + left[:, at + TOP : at + TOP + 1]
            + left[:, at + 2 * TOP : at + 2 * TOP + 1]
        )

    @pl.loop(0, EXPERTS)
    def _(e):
        wanted = (e * CAP).astype(F32)
        here = jnp.zeros((toks, rows), F32)
        weight = jnp.zeros((toks, rows), F32)
        for k in range(TOP):
            hit = diff_ref[k] == wanted
            here = jnp.where(hit, 1.0, here)
            weight = jnp.where(hit, weights[k], weight)
        place = here.astype(BF16)
        scale = jnp.sum(weight, axis=0, keepdims=True)
        place_ref[e] = place
        out_ref[e, :, 0:rows] = jnp.dot(feats, place, preferred_element_type=F32).astype(BF16)
        out_ref[e, :, rows:] = (
            jnp.dot(cots, place, preferred_element_type=F32) * scale
        ).astype(BF16)


def pack(msgs, width):
    toks = msgs.shape[0]
    rows = toks // 2
    return pl.pallas_call(
        pack_kernel,
        out_shape=(
            jax.ShapeDtypeStruct((EXPERTS, width, 2 * rows), BF16),
            jax.ShapeDtypeStruct((EXPERTS, toks, rows), BF16),
        ),
        scratch_shapes=[pltpu.VMEM((TOP, toks, rows), F32)],
        compiler_params=pltpu.CompilerParams(vmem_limit_bytes=VMEM_BYTES),
    )(msgs)


LAST = (((1,), (1,)), ((), ()))
FIRST = (((0,), (0,)), ((), ()))
STEP = 512


def expert_kernel(
    own_ref, oth_ref, wg_ref, wu_ref, wd_ref, gg_ref, gu_ref, gd_ref, keep_ref, send_ref
):
    dim, both = own_ref.shape
    half = both // 2
    units = wg_ref.shape[0]

    def rows_in(at):
        return jnp.concatenate([own_ref[at, :half], oth_ref[at, :half]], axis=1)

    def rows_grad(at):
        return jnp.concatenate([own_ref[at, half:], oth_ref[at, half:]], axis=1)

    def two(at):
        return jnp.concatenate([wg_ref[:, at], wu_ref[:, at]], axis=0)

    fwd = jnp.zeros((2 * units, both), F32)
    grad_act = jnp.zeros((units, both), F32)
    for i in range(dim // STEP):
        at = pl.ds(i * STEP, STEP)
        fwd = fwd + jnp.dot(two(at), rows_in(at), preferred_element_type=F32)
        grad_act = grad_act + jnp.dot(wd_ref[:, at], rows_grad(at), preferred_element_type=F32)
    pre_act, up_value = fwd[:units], fwd[units:]
    sig = jax.nn.sigmoid(pre_act)
    silu = pre_act * sig
    slope = sig * (1.0 + pre_act * (1.0 - sig))
    activation = (silu * up_value).astype(BF16)
    grad_pre = (grad_act * up_value * slope).astype(BF16)
    grad_upv = (grad_act * silu).astype(BF16)
    cots = jnp.concatenate([grad_pre, grad_upv], axis=0)
    for i in range(dim // STEP):
        at = pl.ds(i * STEP, STEP)
        total = lax.dot_general(two(at), cots, FIRST, preferred_element_type=F32)
        keep_ref[at, :] = total[:, :half]
        send_ref[at, :] = total[:, half:].astype(BF16)
        grads = lax.dot_general(cots, rows_in(at), LAST, preferred_element_type=F32).astype(BF16)
        gg_ref[:, at] = grads[:units]
        gu_ref[:, at] = grads[units:]
        gd_ref[:, at] = lax.dot_general(
            activation, rows_grad(at), LAST, preferred_element_type=F32
        ).astype(BF16)


def expert(own, oth, w_gate, w_up, w_down):
    dim, both = own.shape
    grad = jax.ShapeDtypeStruct(w_gate.shape, BF16)
    return pl.pallas_call(
        expert_kernel,
        out_shape=(
            grad,
            grad,
            grad,
            jax.ShapeDtypeStruct((dim, both // 2), F32),
            jax.ShapeDtypeStruct((dim, both // 2), BF16),
        ),
        compiler_params=pltpu.CompilerParams(vmem_limit_bytes=VMEM_BYTES),
    )(own, oth, w_gate, w_up, w_down)


def combine_kernel(back_ref, place_ref, out_ref):
    width, toks = back_ref.shape[1], place_ref.shape[1]

    def add(e, total):
        return total + lax.dot_general(
            back_ref[e], place_ref[e], LAST, preferred_element_type=F32
        )

    total = lax.fori_loop(0, EXPERTS, add, jnp.zeros((width, toks), F32))
    out_ref[...] = jnp.transpose(total)


def combine(back, place):
    return pl.pallas_call(
        combine_kernel,
        out_shape=jax.ShapeDtypeStruct((place.shape[1], back.shape[1]), F32),
        compiler_params=pltpu.CompilerParams(vmem_limit_bytes=VMEM_BYTES),
    )(back, place)


def exchange(value, axis):
    return lax.all_to_all(value, axis, split_axis=0, concat_axis=0, tiled=True)


SWAP = [(0, 1), (1, 0)]


def shards(tokens, grad_out, routes, gate_probs, w_gate, w_up, w_down):
    tok_rows, width = tokens.shape
    dim = w_gate.shape[2]
    w_gate, w_up, w_down = w_gate[0], w_up[0], w_down[0]
    far = exchange(message(tokens, grad_out, routes, gate_probs), "far")
    far = far.reshape(1, FAR * tok_rows, ROW)
    near = exchange(jnp.broadcast_to(far, (NEAR, FAR * tok_rows, ROW)), "near")
    slots, place = pack(near.reshape(NEAR * FAR * tok_rows, ROW), width)
    own = exchange(slots, ("y", "x")).reshape(dim, -1)
    oth = lax.ppermute(own, "core", SWAP)
    grad_gate, grad_up, grad_down, keep, send = expert(own, oth, w_gate, w_up, w_down)
    back = (keep + lax.ppermute(send, "core", SWAP).astype(F32)).astype(BF16)
    back = exchange(back.reshape(EXPERTS, width, -1), ("y", "x"))
    part = combine(back, place)
    part = exchange(part.reshape(NEAR, FAR * tok_rows, width), "near").sum(axis=0)
    part = exchange(part.reshape(FAR, tok_rows, width), "far").sum(axis=0)
    return part.astype(BF16), grad_gate[None], grad_up[None], grad_down[None]


def solution(mesh):
    fine = Mesh(
        mesh.devices.reshape(FAR, NEAR, 2, 4, 4), ("far", "near", "core", "y", "x")
    )
    dp, expert_axes = ("far", "near", "core"), ("y", "x")
    in_specs = (
        P(dp, expert_axes),
        P(dp, expert_axes),
        P(dp, None),
        P(dp, None),
        P(expert_axes, dp, None),
        P(expert_axes, dp, None),
        P(expert_axes, dp, None),
    )
    out_specs = (
        P(dp, expert_axes),
        P(expert_axes, dp, None),
        P(expert_axes, dp, None),
        P(expert_axes, dp, None),
    )
    return jax.shard_map(shards, mesh=fine, in_specs=in_specs, out_specs=out_specs, check_vma=False)
```

time: 570 us -> 175 us (0.31)
  waiting for transfers between devices: 261 us -> 4.9 us
  blocking collectives: 233 us -> 138 us
  other arithmetic: 19.1 us -> 0.83 us
  matrix products: 15.1 us -> 0 us
  between operations: 14.8 us -> 0.71 us
  Pallas kernels: 0 us -> 13.7 us
  local copies, waits for them, and re-layouts: 16.3 us -> 3.9 us
    all_gather x2 -> x0, waiting for transfers between devices: 260 us -> none  [the longest x1 131 us: shards(): lax.all_gather(mine_in, 'dp', axis=0, tiled=True)]
    unnamed x1 -> x0, blocking collectives: 210 us -> none
    all_to_all x2 -> x6, blocking collectives: 23.1 us -> 138 us  [exchange(): return lax.all_to_all(value, axis, split_axis=0, concat_axis=0, tiled=True)]
    unnamed x1 -> x0, other arithmetic: 18 us -> none
    dot_general x11 -> x0, matrix products: 15.1 us -> none  [the longest x1 3.35 us: shards(): jnp.einsum('jfr,rjd->jfd', activation, rows_grad, preferred_element_type=...]
    pallas_call x0 -> x4, Pallas kernels: none -> 13.7 us  [the longest x1 4.71 us: expert(): pl.pallas_call(expert_kernel, out_shape=(grad, grad, grad, jax.ShapeDtype...]
    ppermute x0 -> x2, starting transfers between devices: none -> 10.8 us  [the longest x1 8.48 us: shards(): oth = lax.ppermute(own, 'core', SWAP)]
    all_to_all x1 -> x0, starting transfers between devices: 6.56 us -> none  [shards(): lax.all_to_all(back_rows, 'expert', split_axis=2, concat_axis=1, tiled=True)]
  transfers between devices with their start and end apart: 3 -> 2, of which waited for: 3 -> 2; matrix products, arithmetic and copies ran while one was open for 2% -> 0% of each run, Pallas kernels for 0% -> 0%
where the time goes in v1:
time: 175 us; the launch traced here: 173 us
  blocking collectives  138 us (79%)
  Pallas kernels  13.7 us (8%)
  starting transfers between devices  10.8 us (6%)
  waiting for transfers between devices  4.9 us (3%)
  local copies, waits for them, and re-layouts  3.9 us (2%)
    all_to_all x6, blocking collectives, exchange(): return lax.all_to_all(value, axis, split_axis=0, concat_axis=0, tiled=True)  138 us
    ppermute x1, starting transfers between devices, shards(): oth = lax.ppermute(own, 'core', SWAP)  8.48 us
    pallas_call x1, Pallas kernels, expert(): pl.pallas_call(expert_kernel, out_shape=(grad, grad, grad, jax.ShapeDtype...  4.71 us
    pallas_call x1, Pallas kernels, pack(): pl.pallas_call(pack_kernel, out_shape=(jax.ShapeDtypeStruct((EXPERTS, wid...  4.31 us
    unnamed x10, local copies, waits for them, and re-layouts  3.89 us
  transfers between devices with their start and end apart: 2, of which 2 were waited for; matrix products, arithmetic and copies ran while one was open for 0% of the time, Pallas kernels for 0%

profile of v1, /device:TPU:1, one launch (start us, length us, event | category | flops | bytes accessed | tf_op | source)
XLA Modules:
  0.0 173.0 jit_solution(8812630228929468556)
XLA Ops:
  0.6 1.3 copy.13.routes_ref
  2.0 1.3 copy.14.probs_ref
  3.3 1.6 shard_map.102
  4.9 51.1 %all_to_all.30 = bf16[8,8,512]{2,1,0:T(8,128)(2,1)S(1)} all-to-all(bf16[8,8,512]{2,1,0:T(8,128)(2,1)} %shard_map.102), channel_id=1, replica_groups=mesh['far'=8,'near'=4,'core'=2,'y'=4,'x'=4] {'far'}, dimensions={0} | all-to-all | bytes 131072 | tf_op jit(solution)/shard_map/all_to_all | solution.py:198
  56.1 8.7 %all_to_all.31 = bf16[4,64,512]{2,1,0:T(8,128)(2,1)S(1)} all-to-all(bf16[4,64,512]{2,1,0:T(8,128)(2,1)S(1)} %broadcast_in_dim.17), channel_id=1, replica_groups=mesh['far'=8,'near'=4,'core'=2,'y'=4,'x'=4] {'near'}, dimensions={0} | all-to-all | bytes 524288 | tf_op jit(solution)/shard_map/all_to_all | solution.py:198
  64.8 4.3 %shard_map.103 = (bf16[16,192,256]{2,1,0:T(8,128)(2,1)S(1)}, bf16[16,256,128]{2,1,0:T(8,128)(2,1)S(1)}) custom-call(bf16[256,512]{1,0:T(8,128)(2,1)S(1)} %bitcast.14), custom_call_target="tpu_custom_call" | custom-call | tf_op jit(solution)/shard_map/pallas_call | solution.py:102
  69.1 0.0 copy-start
  69.1 0.0 copy-start.1
  69.1 0.0 copy-start.2
  69.1 24.0 %all_to_all.32 = bf16[16,192,256]{2,1,0:T(8,128)(2,1)S(1)} all-to-all(bf16[16,192,256]{2,1,0:T(8,128)(2,1)S(1)} %get-tuple-element.11), channel_id=1, replica_groups=mesh['far'=8,'near'=4,'core'=2,'y'=4,'x'=4] {'y','x'}, dimensions={0} | all-to-all | bytes 3145728 | tf_op jit(solution)/shard_map/all_to_all | solution.py:198
  93.1 8.5 %collective-permute-start = (bf16[3072,256]{1,0:T(8,128)(2,1)S(1)}, bf16[3072,256]{1,0:T(8,128)(2,1)S(1)}, u32[]{:S(2)}, u32[]{:S(2)}) collective-permute-start(bf16[3072,256]{1,0:T(8,128)(2,1)S(1)} %bitcast.12), channel_id=1, source_target_pairs={{0,16},{16,0},{1,17},{17,1},{2,18},{18,2},{3,19},{19,3},{4,20},{20... | collective-permute-start | bytes 4718600 | tf_op jit(solution)/shard_map/ppermute | solution.py:213
  101.6 3.0 %collective-permute-done.oth_ref = bf16[3072,256]{1,0:T(8,128)(2,1)S(1)} collective-permute-done((bf16[3072,256]{1,0:T(8,128)(2,1)S(1)}, bf16[3072,256]{1,0:T(8,128)(2,1)S(1)}, u32[]{:S(2)}, u32[]{:S(2)}) %collective-permute-start) | collective-permute-done | bytes 1572896 | tf_op jit(solution)/shard_map/ppermute | solution.py:213
  104.6 1.2 copy-done.3
  105.8 0.0 copy-done
  105.8 0.0 copy-done.1
  105.8 4.7 %shard_map.104 = (bf16[96,3072]{1,0:T(8,128)(2,1)}, bf16[96,3072]{1,0:T(8,128)(2,1)}, bf16[96,3072]{1,0:T(8,128)(2,1)}, f32[3072,128]{1,0:T(8,128)S(1)}, bf16[3072,128]{1,0:T(8,128)(2,1)S(1)}) custom-call(bf16[3072,256]{1,0:T(8,128)(2,1)S(1)} %bitcast.13, bf16[3072,256]{1,0:T(8,128)(2,1)} %copy-done.3, bf16[96,3072]{1,0:T(8,128)(2,1)S(1)} %bitcast.16, ...), custom_call_target="tpu_custom_call" | custom-call | tf_op jit(solution)/shard_map/pallas_call | solution.py:164
  110.5 2.3 %collective-permute-start.1 = (bf16[3072,128]{1,0:T(8,128)(2,1)S(1)}, bf16[3072,128]{1,0:T(8,128)(2,1)S(1)}, u32[]{:S(2)}, u32[]{:S(2)}) collective-permute-start(bf16[3072,128]{1,0:T(8,128)(2,1)S(1)} %get-tuple-element.13), channel_id=1, source_target_pairs={{0,16},{16,0},{1,17},{17,1},{2,18},{18,2},{3,19},{19,3},{4,20},{20... | collective-permute-start | bytes 2359304 | tf_op jit(solution)/shard_map/ppermute | solution.py:215
  112.8 1.9 %collective-permute-done.1 = bf16[3072,128]{1,0:T(8,128)(2,1)S(1)} collective-permute-done((bf16[3072,128]{1,0:T(8,128)(2,1)S(1)}, bf16[3072,128]{1,0:T(8,128)(2,1)S(1)}, u32[]{:S(2)}, u32[]{:S(2)}) %collective-permute-start.1) | collective-permute-done | bytes 786464 | tf_op jit(solution)/shard_map/ppermute | solution.py:215
  114.7 0.2 add_convert_fusion
  114.9 16.5 %all_to_all.33.back_ref = bf16[16,192,128]{2,1,0:T(8,128)(2,1)S(1)} all-to-all(bf16[16,192,128]{2,1,0:T(8,128)(2,1)S(1)} %bitcast.19), channel_id=1, replica_groups=mesh['far'=8,'near'=4,'core'=2,'y'=4,'x'=4] {'y','x'}, dimensions={0} | all-to-all | bytes 1572864 | tf_op jit(solution)/shard_map/all_to_all | solution.py:198
  131.5 3.1 %shard_map.105 = f32[256,192]{1,0:T(8,128)S(1)} custom-call(bf16[16,192,128]{2,1,0:T(8,128)(2,1)S(1)} %all_to_all.33.back_ref, bf16[16,256,128]{2,1,0:T(8,128)(2,1)S(1)} %get-tuple-element.14.place_ref), custom_call_target="tpu_custom_call" | custom-call | tf_op jit(solution)/shard_map/pallas_call | solution.py:190
  134.6 8.6 %all_to_all.34 = f32[4,64,192]{2,1,0:T(8,128)S(1)} all-to-all(f32[4,64,192]{2,1,0:T(8,128)S(1)} %bitcast.15), channel_id=1, replica_groups=mesh['far'=8,'near'=4,'core'=2,'y'=4,'x'=4] {'near'}, dimensions={0} | all-to-all | bytes 393216 | tf_op jit(solution)/shard_map/all_to_all | solution.py:198
  143.2 29.2 %all_to_all.35 = f32[8,8,192]{2,1,0:T(8,128)S(1)} all-to-all(f32[8,8,192]{2,1,0:T(8,128)S(1)} %bitcast.21), channel_id=1, replica_groups=mesh['far'=8,'near'=4,'core'=2,'y'=4,'x'=4] {'far'}, dimensions={0} | all-to-all | bytes 98304 | tf_op jit(solution)/shard_map/all_to_all | solution.py:198
  172.4 0.6 reduce_sum.19
  (4 shorter events, 0.0 us)
Async XLA Ops:
  69.1 36.7 %copy-start = (bf16[1,96,3072]{2,1,0:T(8,128)(2,1)S(1)}, bf16[1,96,3072]{2,1,0:T(8,128)(2,1)}, u32[]{:S(2)}) copy-start(bf16[1,96,3072]{2,1,0:T(8,128)(2,1)} %param.11) | copy-start | bytes 1769476
  69.1 36.7 %copy-start.1 = (bf16[1,96,3072]{2,1,0:T(8,128)(2,1)S(1)}, bf16[1,96,3072]{2,1,0:T(8,128)(2,1)}, u32[]{:S(2)}) copy-start(bf16[1,96,3072]{2,1,0:T(8,128)(2,1)} %param.12) | copy-start | bytes 1769476
  69.1 36.7 %copy-start.2 = (bf16[1,96,3072]{2,1,0:T(8,128)(2,1)S(1)}, bf16[1,96,3072]{2,1,0:T(8,128)(2,1)}, u32[]{:S(2)}) copy-start(bf16[1,96,3072]{2,1,0:T(8,128)(2,1)} %param.13) | copy-start | bytes 1769476
  93.1 11.5 %collective-permute-start = (bf16[3072,256]{1,0:T(8,128)(2,1)S(1)}, bf16[3072,256]{1,0:T(8,128)(2,1)S(1)}, u32[]{:S(2)}, u32[]{:S(2)}) collective-permute-start(bf16[3072,256]{1,0:T(8,128)(2,1)S(1)} %bitcast.12), channel_id=1, source_target_pairs={{0,16},{16,0},{1,17},{17,1},{2,18},{18,2},{3,19},{19,3},{4,20},{20... | collective-permute-start | bytes 4718600 | tf_op jit(solution)/shard_map/ppermute | solution.py:213
  104.6 1.2 copy-start.3
  110.5 4.2 %collective-permute-start.1 = (bf16[3072,128]{1,0:T(8,128)(2,1)S(1)}, bf16[3072,128]{1,0:T(8,128)(2,1)S(1)}, u32[]{:S(2)}, u32[]{:S(2)}) collective-permute-start(bf16[3072,128]{1,0:T(8,128)(2,1)S(1)} %get-tuple-element.13), channel_id=1, source_target_pairs={{0,16},{16,0},{1,17},{17,1},{2,18},{18,2},{3,19},{19,3},{4,20},{20... | collective-permute-start | bytes 2359304 | tf_op jit(solution)/shard_map/ppermute | solution.py:215

commit v2 on v1

v2 whole, which is shorter than its diff:
```python
import jax
import jax.numpy as jnp
from jax import lax
from jax.experimental import pallas as pl
from jax.experimental.pallas import tpu as pltpu
from jax.sharding import Mesh, PartitionSpec as P

EXPERTS = 16
CAP = 4
TOP = 4
FAR = 16
PAIR = 2
BF16 = jnp.bfloat16
F32 = jnp.float32
VMEM_BYTES = 24 * 1024 * 1024
LAST = (((1,), (1,)), ((), ()))
FIRST = (((0,), (0,)), ((), ()))
GRAD_AT = 256
ROW = 512
STEP = 384


def iota(shape, dim):
    return lax.broadcasted_iota(jnp.int32, shape, dim)


def message_kernel(tokens_ref, grad_ref, routes_ref, probs_ref, out_ref):
    tok_rows, width = tokens_ref.shape
    eye = iota((tok_rows, tok_rows), 0) == iota((tok_rows, tok_rows), 1)

    def column(values):
        spread = jnp.broadcast_to(values, (tok_rows, tok_rows))
        return jnp.sum(jnp.where(eye, spread, 0.0), axis=1, keepdims=True)

    lane = iota((tok_rows, 128), 1)
    row = iota((tok_rows, 128), 0)
    expert_at = (lane & (EXPERTS - 1)).astype(F32)
    chosen = jnp.zeros((tok_rows, 128), F32)
    weight = jnp.zeros((tok_rows, 128), F32)
    for k in range(TOP):
        hit = expert_at == column(routes_ref[k : k + 1, :].astype(F32))
        chosen = jnp.where(hit, 1.0, chosen)
        weight = jnp.where(hit, column(probs_ref[k : k + 1, :]), weight)
    before = jnp.zeros((tok_rows, 128), F32)
    for s in range(1, tok_rows):
        before = before + jnp.where(row >= s, pltpu.roll(chosen, s, 0), 0.0)
    kind = lane >> 4
    meta = jnp.where(kind == 4, jnp.where(chosen > 0.0, before, -1.0), 0.0)
    rest = weight
    for part in range(3):
        piece = rest.astype(BF16).astype(F32)
        meta = jnp.where(kind == 5 + part, piece, meta)
        rest = rest - piece
    meta = meta.astype(BF16)
    blank = jnp.zeros((tok_rows, 128), BF16)
    for copy in range(out_ref.shape[0]):
        out_ref[copy, :, 128:256] = meta
        out_ref[copy, :, 0:width] = tokens_ref[...]
        out_ref[copy, :, GRAD_AT + 128 : ROW] = blank
        out_ref[copy, :, GRAD_AT : GRAD_AT + width] = grad_ref[...]


def message(tokens, grad_out, routes, probs):
    return pl.pallas_call(
        message_kernel,
        out_shape=jax.ShapeDtypeStruct((FAR, tokens.shape[0], ROW), BF16),
    )(tokens, grad_out, routes.T, probs.T)


def pack_kernel(pair_ref, msg_ref, out_ref, table_ref):
    toks = msg_ref.shape[0]
    width, lanes = out_ref.shape[1:]
    half = lanes // 2
    left = msg_ref[:, 0:GRAD_AT].astype(F32)
    left_t = jnp.transpose(left)
    right_t = jnp.transpose(msg_ref[:, GRAD_AT:ROW].astype(F32))
    table_ref[...] = left_t[width : width + EXPERTS]
    top = jnp.concatenate([left_t[:width], right_t[:width]], axis=1)
    parts = left_t[width + EXPERTS : width + 4 * EXPERTS]
    low = jnp.concatenate([jnp.zeros_like(parts), parts], axis=1)
    lhs = jnp.concatenate([top, low], axis=0).astype(BF16)
    pair = pair_ref[0]
    tok = iota((2 * toks, lanes), 0)
    lane = iota((2 * toks, lanes), 1)
    row = lane & (half - 1)
    is_in = (lane >= half) == (pair == 1)
    fits = (((tok & (toks - 1)) >> 3) == (row >> 2)) & ((tok < toks) == is_in)
    wanted = jnp.where(fits, (row & 3).astype(F32), 9.0)
    in_lane = (iota((1, lanes), 1) >= half) == (pair == 1)
    for e in range(0, EXPERTS, 2):
        places = []
        for j in (e, e + 1):
            slot = left[:, width + j : width + j + 1]
            slot = jnp.concatenate([slot, slot], axis=0)
            places.append(jnp.where(slot == wanted, 1.0, 0.0))
        place = jnp.concatenate(places, axis=1).astype(BF16)
        both = jnp.dot(lhs, place, preferred_element_type=F32)
        for j in (0, 1):
            block = both[:, j * lanes : (j + 1) * lanes]
            scale = block[width + e + j : width + e + j + 1]
            for part in (1, 2):
                at = width + part * EXPERTS + e + j
                scale = scale + block[at : at + 1]
            scale = jnp.where(in_lane, 1.0, scale)
            packed = (block[:width] * scale).astype(BF16)
            for p in range(PAIR):
                out_ref[p * EXPERTS + e + j] = packed


def pack(pair, msgs, width):
    toks = msgs.shape[0]
    return pl.pallas_call(
        pack_kernel,
        in_specs=[
            pl.BlockSpec(memory_space=pltpu.SMEM),
            pl.BlockSpec(memory_space=pltpu.VMEM),
        ],
        out_shape=(
            jax.ShapeDtypeStruct((PAIR * EXPERTS, width, toks), BF16),
            jax.ShapeDtypeStruct((EXPERTS, toks), F32),
        ),
        compiler_params=pltpu.CompilerParams(vmem_limit_bytes=VMEM_BYTES),
    )(pair, msgs)


def rows_at(own_ref, oth_ref, at):
    lanes = own_ref.shape[2]
    first = iota((at.size, lanes), 1) < lanes // 2
    ins, cots = [], []
    for ref in (own_ref, oth_ref):
        even, odd = ref[0, at, :], ref[1, at, :]
        ins.append(jnp.where(first, even, odd))
        cots.append(jnp.where(first, odd, even))
    return jnp.concatenate(ins, axis=1), jnp.concatenate(cots, axis=1)


def turn(value, lanes):
    blocks = [
        pltpu.roll(value[:, at : at + lanes], lanes // 2, 1)
        for at in range(0, value.shape[1], lanes)
    ]
    return jnp.concatenate(blocks, axis=1)


def expert_kernel(
    own_ref, oth_ref, wg_ref, wu_ref, wd_ref, keep_ref, send_ref, cots_ref, act_ref
):
    dim, lanes = own_ref.shape[1:]
    units = wg_ref.shape[0]
    width = keep_ref.shape[2] * 2

    def two(at):
        return jnp.concatenate([wg_ref[:, at], wu_ref[:, at]], axis=0)

    fwd = jnp.zeros((2 * units, 2 * lanes), F32)
    grad_act = jnp.zeros((units, 2 * lanes), F32)
    for i in range(dim // STEP):
        at = pl.ds(i * STEP, STEP)
        rows_in, rows_grad = rows_at(own_ref, oth_ref, at)
        fwd = fwd + jnp.dot(two(at), rows_in, preferred_element_type=F32)
        grad_act = grad_act + jnp.dot(wd_ref[:, at], rows_grad, preferred_element_type=F32)
    grad_act = turn(grad_act, lanes)
    pre_act, up_value = fwd[:units], fwd[units:]
    sig = jax.nn.sigmoid(pre_act)
    silu = pre_act * sig
    slope = sig * (1.0 + pre_act * (1.0 - sig))
    act_ref[...] = turn(silu * up_value, lanes).astype(BF16)
    grad_pre = (grad_act * up_value * slope).astype(BF16)
    grad_upv = (grad_act * silu).astype(BF16)
    cots = jnp.concatenate([grad_pre, grad_upv], axis=0)
    cots_ref[...] = cots
    first = iota((width // 2, lanes), 1) < lanes // 2
    for i in range(dim // STEP):
        at = pl.ds(i * STEP, STEP)
        total = lax.dot_general(two(at), cots, FIRST, preferred_element_type=F32)
        for j in range(STEP // width):
            e = i * (STEP // width) + j
            for ref, begin in ((keep_ref, 0), (send_ref, lanes)):
                block = total[j * width : (j + 1) * width, begin : begin + lanes]
                upper, lower = block[: width // 2], block[width // 2 :]
                even = jnp.where(first, upper, pltpu.roll(lower, lanes // 2, 1))
                odd = jnp.where(first, pltpu.roll(upper, lanes // 2, 1), lower)
                ref[0, e] = even.astype(ref.dtype)
                ref[1, e] = odd.astype(ref.dtype)


def expert(own, oth, w_gate, w_up, w_down, width):
    units, dim = w_gate.shape
    lanes = own.shape[2]
    back = (PAIR, EXPERTS, width // 2, lanes)
    return pl.pallas_call(
        expert_kernel,
        out_shape=(
            jax.ShapeDtypeStruct(back, F32),
            jax.ShapeDtypeStruct(back, BF16),
            jax.ShapeDtypeStruct((2 * units, 2 * lanes), BF16),
            jax.ShapeDtypeStruct((units, 2 * lanes), BF16),
        ),
        cost_estimate=pl.CostEstimate(
            flops=2 * 5 * units * dim * 2 * lanes, bytes_accessed=9 << 20, transcendentals=0
        ),
        compiler_params=pltpu.CompilerParams(vmem_limit_bytes=VMEM_BYTES),
    )(own, oth, w_gate, w_up, w_down)


def grads_kernel(own_ref, oth_ref, cots_ref, act_ref, gg_ref, gu_ref, gd_ref):
    units, dim = gg_ref.shape
    for i in range(dim // STEP):
        at = pl.ds(i * STEP, STEP)
        rows_in, rows_grad = rows_at(own_ref, oth_ref, at)
        grads = lax.dot_general(cots_ref[...], rows_in, LAST, preferred_element_type=F32)
        grads = grads.astype(BF16)
        gg_ref[:, at] = grads[:units]
        gu_ref[:, at] = grads[units:]
        gd_ref[:, at] = lax.dot_general(
            act_ref[...], rows_grad, LAST, preferred_element_type=F32
        ).astype(BF16)


def weight_grads(own, oth, cots, act):
    units, dim = act.shape[0], own.shape[1]
    grad = jax.ShapeDtypeStruct((units, dim), BF16)
    return pl.pallas_call(
        grads_kernel,
        out_shape=(grad, grad, grad),
        cost_estimate=pl.CostEstimate(
            flops=2 * 3 * units * dim * act.shape[1], bytes_accessed=5 << 20, transcendentals=0
        ),
        compiler_params=pltpu.CompilerParams(vmem_limit_bytes=VMEM_BYTES),
    )(own, oth, cots, act)


def combine_kernel(back_ref, table_ref, out_ref):
    height, lanes = back_ref.shape[1:]
    toks = table_ref.shape[1]
    half = lanes // 2
    row = iota((lanes, 2 * toks), 0)
    col = iota((lanes, 2 * toks), 1)
    slot_row = row & (half - 1)
    fits = ((row >= half) == (col >= toks)) & (((col & (toks - 1)) >> 3) == (slot_row >> 2))
    wanted = jnp.where(fits, (slot_row & 3).astype(F32), 9.0)
    total = jnp.zeros((2 * height, 2 * toks), F32)
    for e in range(0, EXPERTS, 2):
        places = []
        for j in (e, e + 1):
            slot = table_ref[j : j + 1, :]
            slot = jnp.concatenate([slot, slot], axis=1)
            places.append(jnp.where(slot == wanted, 1.0, 0.0))
        place = jnp.concatenate(places, axis=0).astype(BF16)
        rows = [
            jnp.concatenate([back_ref[p * EXPERTS + e], back_ref[p * EXPERTS + e + 1]], axis=1)
            for p in range(PAIR)
        ]
        total = total + jnp.dot(
            jnp.concatenate(rows, axis=0), place, preferred_element_type=F32
        )
    total = total[:height] + total[height:]
    total = jnp.concatenate([total[:, :toks], total[:, toks:]], axis=0)
    pad = jnp.zeros((out_ref.shape[1] - 2 * height, toks), F32)
    out_ref[...] = jnp.transpose(jnp.concatenate([total, pad], axis=0)).astype(BF16)


def combine(back, table):
    return pl.pallas_call(
        combine_kernel,
        out_shape=jax.ShapeDtypeStruct((table.shape[1], 256), BF16),
        compiler_params=pltpu.CompilerParams(vmem_limit_bytes=VMEM_BYTES),
    )(back, table)


def sum_kernel(parts_ref, out_ref):
    total = parts_ref[0].astype(F32)
    for i in range(1, parts_ref.shape[0]):
        total = total + parts_ref[i].astype(F32)
    out_ref[...] = total[:, : out_ref.shape[1]].astype(BF16)


def add_parts(parts, width):
    return pl.pallas_call(
        sum_kernel, out_shape=jax.ShapeDtypeStruct((parts.shape[1], width), BF16)
    )(parts)


def exchange(value, axis):
    return lax.all_to_all(value, axis, split_axis=0, concat_axis=0, tiled=True)


SWAP = [(0, 1), (1, 0)]
WIDE = ("pair", "y", "x")


def shards(tokens, grad_out, routes, gate_probs, w_gate, w_up, w_down):
    tok_rows, width = tokens.shape
    dim = w_gate.shape[2]
    w_gate, w_up, w_down = w_gate[0], w_up[0], w_down[0]
    pair = lax.axis_index("pair").astype(jnp.int32).reshape(1)
    far = exchange(message(tokens, grad_out, routes, gate_probs), "far")
    slots, table = pack(pair, far.reshape(FAR * tok_rows, ROW), width)
    own = exchange(slots, WIDE).reshape(PAIR, dim, -1)
    oth = lax.ppermute(own, "core", SWAP)
    keep, send, cots, act = expert(own, oth, w_gate, w_up, w_down, width)
    back = (keep + lax.ppermute(send, "core", SWAP).astype(F32)).astype(BF16)
    back = exchange(back.reshape((PAIR * EXPERTS,) + back.shape[2:]), WIDE)
    part = combine(back, table)
    part = exchange(part.reshape(FAR, tok_rows, part.shape[1]), "far")
    grad_in = add_parts(part, width)
    grad_gate, grad_up, grad_down = weight_grads(own, oth, cots, act)
    return grad_in, grad_gate[None], grad_up[None], grad_down[None]


def solution(mesh):
    fine = Mesh(
        mesh.devices.reshape(FAR, PAIR, 2, 4, 4), ("far", "pair", "core", "y", "x")
    )
    dp, expert_axes = ("far", "pair", "core"), ("y", "x")
    in_specs = (
        P(dp, expert_axes),
        P(dp, expert_axes),
        P(dp, None),
        P(dp, None),
        P(expert_axes, dp, None),
        P(expert_axes, dp, None),
        P(expert_axes, dp, None),
    )
    out_specs = (
        P(dp, expert_axes),
        P(expert_axes, dp, None),
        P(expert_axes, dp, None),
        P(expert_axes, dp, None),
    )
    return jax.shard_map(shards, mesh=fine, in_specs=in_specs, out_specs=out_specs, check_vma=False)
```

time: 175 us -> 151 us (0.86)
  blocking collectives: 138 us -> 40.2 us
  waiting for transfers between devices: 4.9 us -> 46.7 us
  starting transfers between devices: 10.8 us -> 51.6 us
  Pallas kernels: 13.7 us -> 9.05 us
  local copies, waits for them, and re-layouts: 3.9 us -> 0.65 us
    all_to_all x6 -> x2, blocking collectives: 138 us -> 40.2 us  [exchange(): return lax.all_to_all(value, axis, split_axis=0, concat_axis=0, tiled=True)]
    all_to_all x0 -> x2, waiting for transfers between devices: none -> 41.8 us  [exchange(): return lax.all_to_all(value, axis, split_axis=0, concat_axis=0, tiled=True)]
    all_to_all x0 -> x2, starting transfers between devices: none -> 40.8 us  [exchange(): return lax.all_to_all(value, axis, split_axis=0, concat_axis=0, tiled=True)]
    pallas_call x3 -> x5, Pallas kernels: 12.1 us -> 7.56 us  [the longest x1 2.27 us: weight_grads(): pl.pallas_call(grads_kernel, out_shape=(grad, grad, grad), cost_estimate=...]
    unnamed x10 -> x8, local copies, waits for them, and re-layouts: 3.89 us -> 0.65 us
  transfers between devices with their start and end apart: 2 -> 4, of which waited for: 2 -> 4; matrix products, arithmetic and copies ran while one was open for 0% -> 0% of each run, Pallas kernels for 0% -> 2%
where the time goes in v2:
time: 151 us; the launch traced here: 149 us
  starting transfers between devices  51.6 us (34%)
  waiting for transfers between devices  46.7 us (31%)
  blocking collectives  40.2 us (27%)
  Pallas kernels  9.05 us (6%)
    all_to_all x2, waiting for transfers between devices, exchange(): return lax.all_to_all(value, axis, split_axis=0, concat_axis=0, tiled=True)  41.8 us
    all_to_all x2, starting transfers between devices, exchange(): return lax.all_to_all(value, axis, split_axis=0, concat_axis=0, tiled=True)  40.8 us
    all_to_all x2, blocking collectives, exchange(): return lax.all_to_all(value, axis, split_axis=0, concat_axis=0, tiled=True)  40.2 us
    ppermute x1, starting transfers between devices, shards(): oth = lax.ppermute(own, 'core', SWAP)  8.43 us
  transfers between devices with their start and end apart: 4, of which 4 were waited for; matrix products, arithmetic and copies ran while one was open for 0% of the time, Pallas kernels for 2%

profile of v2, /device:TPU:1, one launch (start us, length us, event | category | flops | bytes accessed | tf_op | source)
XLA Modules:
  0.0 149.0 jit_solution(24970054458019525)
XLA Ops:
  0.6 1.5 shard_map.102
  2.1 29.0 %all-to-all-start = ((bf16[16,8,512]{2,1,0:T(8,128)(2,1)}), bf16[16,8,512]{2,1,0:T(8,128)(2,1)S(1)}, u32[]{:S(2)}, u32[]{:S(2)}) async-start(bf16[16,8,512]{2,1,0:T(8,128)(2,1)} %shard_map.102), calls=%async_computation | async-start | bytes 262144 | tf_op jit(solution)/shard_map/all_to_all | solution.py:285
  31.1 22.1 %all-to-all-done = bf16[16,8,512]{2,1,0:T(8,128)(2,1)S(1)} async-done(((bf16[16,8,512]{2,1,0:T(8,128)(2,1)}), bf16[16,8,512]{2,1,0:T(8,128)(2,1)S(1)}, u32[]{:S(2)}, u32[]{:S(2)}) %all-to-all-start) | async-done | bytes 131104 | tf_op jit(solution)/shard_map/all_to_all | solution.py:285
  53.2 0.6 shard_map.103
  53.9 0.0 copy-start
  53.9 0.0 copy-start.1
  53.9 0.0 copy-start.2
  53.9 24.3 %all_to_all.20 = bf16[32,192,128]{2,1,0:T(8,128)(2,1)S(1)} all-to-all(bf16[32,192,128]{2,1,0:T(8,128)(2,1)S(1)} %get-tuple-element.13), channel_id=1, replica_groups=mesh['far'=16,'pair'=2,'core'=2,'y'=4,'x'=4] {'pair','y','x'}, dimensions={0} | all-to-all | bytes 3145728 | tf_op jit(solution)/shard_map/all_to_all | solution.py:285
  78.2 8.4 %collective-permute-start = (bf16[2,3072,128]{2,1,0:T(8,128)(2,1)S(1)}, bf16[2,3072,128]{2,1,0:T(8,128)(2,1)S(1)}, u32[]{:S(2)}, u32[]{:S(2)}) collective-permute-start(bf16[2,3072,128]{2,1,0:T(8,128)(2,1)S(1)} %bitcast.13), channel_id=1, source_target_pairs={{0,16},{16,0},{1,17},{17,1},{2,18},{18,2},{3,19},{19,3},{4,20},{20... | collective-permute-start | bytes 4718600 | tf_op jit(solution)/shard_map/ppermute | solution.py:300
  86.6 3.0 %collective-permute-done.oth_ref = bf16[2,3072,128]{2,1,0:T(8,128)(2,1)S(1)} collective-permute-done((bf16[2,3072,128]{2,1,0:T(8,128)(2,1)S(1)}, bf16[2,3072,128]{2,1,0:T(8,128)(2,1)S(1)}, u32[]{:S(2)}, u32[]{:S(2)}) %collective-permute-start) | collective-permute-done | bytes 1572896 | tf_op jit(solution)/shard_map/ppermute | solution.py:300
  89.7 0.0 copy-done
  89.7 0.0 copy-done.1
  89.7 0.0 copy-done.2
  89.7 2.1 %shard_map.104 = (f32[2,16,96,128]{3,2,1,0:T(8,128)S(1)}, bf16[2,16,96,128]{3,2,1,0:T(8,128)(2,1)S(1)}, bf16[192,256]{1,0:T(8,128)(2,1)S(1)}, bf16[96,256]{1,0:T(8,128)(2,1)S(1)}) custom-call(bf16[2,3072,128]{2,1,0:T(8,128)(2,1)S(1)} %bitcast.14, bf16[2,3072,128]{2,1,0:T(8,128)(2,1)S(1)} %collective-permute-done.oth_ref, bf16[96,3072]{1,0:T(8,128)(2,1)S(1)} %bitcast.16, ...), custom_call_target="tpu_custom_call" | custom-call | flops 754974720 | bytes 9437184 | tf_op jit(solution)/shard_map/pallas_call | solution.py:191
  91.8 2.3 %collective-permute-start.1 = (bf16[2,16,96,128]{3,2,1,0:T(8,128)(2,1)S(1)}, bf16[2,16,96,128]{3,2,1,0:T(8,128)(2,1)S(1)}, u32[]{:S(2)}, u32[]{:S(2)}) collective-permute-start(bf16[2,16,96,128]{3,2,1,0:T(8,128)(2,1)S(1)} %get-tuple-element.15), channel_id=1, source_target_pairs={{0,16},{16,0},{1,17},{17,1},{2,18},{18,2},{3,19},{19,3},{4,20},{20... | collective-permute-start | bytes 2359304 | tf_op jit(solution)/shard_map/ppermute | solution.py:302
  94.1 1.9 %collective-permute-done.1 = bf16[2,16,96,128]{3,2,1,0:T(8,128)(2,1)S(1)} collective-permute-done((bf16[2,16,96,128]{3,2,1,0:T(8,128)(2,1)S(1)}, bf16[2,16,96,128]{3,2,1,0:T(8,128)(2,1)S(1)}, u32[]{:S(2)}, u32[]{:S(2)}) %collective-permute-start.1) | collective-permute-done | bytes 786464 | tf_op jit(solution)/shard_map/ppermute | solution.py:302
  96.0 0.2 add_convert_fusion
  96.1 15.9 %all_to_all.21.back_ref = bf16[32,96,128]{2,1,0:T(8,128)(2,1)S(1)} all-to-all(bf16[32,96,128]{2,1,0:T(8,128)(2,1)S(1)} %bitcast.20), channel_id=1, replica_groups=mesh['far'=16,'pair'=2,'core'=2,'y'=4,'x'=4] {'pair','y','x'}, dimensions={0} | all-to-all | bytes 1572864 | tf_op jit(solution)/shard_map/all_to_all | solution.py:285
  112.1 1.1 shard_map.105
  113.2 11.8 %all-to-all-start.3 = ((bf16[16,8,256]{2,1,0:T(8,128)(2,1)}), bf16[16,8,256]{2,1,0:T(8,128)(2,1)S(1)}, u32[]{:S(2)}, u32[]{:S(2)}) async-start(bf16[16,8,256]{2,1,0:T(8,128)(2,1)} %bitcast.9), calls=%async_computation.3 | async-start | bytes 131072 | tf_op jit(solution)/shard_map/all_to_all | solution.py:285
  125.0 2.3 %shard_map.107 = (bf16[96,3072]{1,0:T(8,128)(2,1)}, bf16[96,3072]{1,0:T(8,128)(2,1)}, bf16[96,3072]{1,0:T(8,128)(2,1)}) custom-call(bf16[2,3072,128]{2,1,0:T(8,128)(2,1)S(1)} %bitcast.15, bf16[2,3072,128]{2,1,0:T(8,128)(2,1)S(1)} %collective-permute-done.oth_ref, bf16[192,256]{1,0:T(8,128)(2,1)S(1)} %get-tuple-element.17.cots_ref, ...), custom_call_target="tpu_custom_call" | custom-call | flops 452984832 | bytes 5242880 | tf_op jit(solution)/shard_map/pallas_call | solution.py:223
  127.3 19.7 %all-to-all-done.3.parts_ref = bf16[16,8,256]{2,1,0:T(8,128)(2,1)S(1)} async-done(((bf16[16,8,256]{2,1,0:T(8,128)(2,1)}), bf16[16,8,256]{2,1,0:T(8,128)(2,1)S(1)}, u32[]{:S(2)}, u32[]{:S(2)}) %all-to-all-start.3) | async-done | bytes 65568 | tf_op jit(solution)/shard_map/all_to_all | solution.py:285
  147.0 0.6 copy-done.3
  147.6 1.4 shard_map.106
  (1 shorter events, 0.0 us)
Async XLA Ops:
  2.1 51.1 %all-to-all-start = ((bf16[16,8,512]{2,1,0:T(8,128)(2,1)}), bf16[16,8,512]{2,1,0:T(8,128)(2,1)S(1)}, u32[]{:S(2)}, u32[]{:S(2)}) async-start(bf16[16,8,512]{2,1,0:T(8,128)(2,1)} %shard_map.102), calls=%async_computation | async-start | bytes 262144 | tf_op jit(solution)/shard_map/all_to_all | solution.py:285
  53.9 35.8 %copy-start = (bf16[1,96,3072]{2,1,0:T(8,128)(2,1)S(1)}, bf16[1,96,3072]{2,1,0:T(8,128)(2,1)}, u32[]{:S(2)}) copy-start(bf16[1,96,3072]{2,1,0:T(8,128)(2,1)} %param.11) | copy-start | bytes 1769476
  53.9 35.8 %copy-start.1 = (bf16[1,96,3072]{2,1,0:T(8,128)(2,1)S(1)}, bf16[1,96,3072]{2,1,0:T(8,128)(2,1)}, u32[]{:S(2)}) copy-start(bf16[1,96,3072]{2,1,0:T(8,128)(2,1)} %param.12) | copy-start | bytes 1769476
  53.9 35.8 %copy-start.2 = (bf16[1,96,3072]{2,1,0:T(8,128)(2,1)S(1)}, bf16[1,96,3072]{2,1,0:T(8,128)(2,1)}, u32[]{:S(2)}) copy-start(bf16[1,96,3072]{2,1,0:T(8,128)(2,1)} %param.13) | copy-start | bytes 1769476
  78.2 11.5 %collective-permute-start = (bf16[2,3072,128]{2,1,0:T(8,128)(2,1)S(1)}, bf16[2,3072,128]{2,1,0:T(8,128)(2,1)S(1)}, u32[]{:S(2)}, u32[]{:S(2)}) collective-permute-start(bf16[2,3072,128]{2,1,0:T(8,128)(2,1)S(1)} %bitcast.13), channel_id=1, source_target_pairs={{0,16},{16,0},{1,17},{17,1},{2,18},{18,2},{3,19},{19,3},{4,20},{20... | collective-permute-start | bytes 4718600 | tf_op jit(solution)/shard_map/ppermute | solution.py:300
  91.8 4.2 %collective-permute-start.1 = (bf16[2,16,96,128]{3,2,1,0:T(8,128)(2,1)S(1)}, bf16[2,16,96,128]{3,2,1,0:T(8,128)(2,1)S(1)}, u32[]{:S(2)}, u32[]{:S(2)}) collective-permute-start(bf16[2,16,96,128]{3,2,1,0:T(8,128)(2,1)S(1)} %get-tuple-element.15), channel_id=1, source_target_pairs={{0,16},{16,0},{1,17},{17,1},{2,18},{18,2},{3,19},{19,3},{4,20},{20... | collective-permute-start | bytes 2359304 | tf_op jit(solution)/shard_map/ppermute | solution.py:302
  113.2 33.8 %all-to-all-start.3 = ((bf16[16,8,256]{2,1,0:T(8,128)(2,1)}), bf16[16,8,256]{2,1,0:T(8,128)(2,1)S(1)}, u32[]{:S(2)}, u32[]{:S(2)}) async-start(bf16[16,8,256]{2,1,0:T(8,128)(2,1)} %bitcast.9), calls=%async_computation.3 | async-start | bytes 131072 | tf_op jit(solution)/shard_map/all_to_all | solution.py:285
  146.9 0.6 copy-start.3

commit v3 on v2

--- a/solution.py
+++ b/solution.py
@@ -123,48 +123,43 @@
     )(pair, msgs)
 
 
-def rows_at(own_ref, oth_ref, at):
+def rows_at(own_ref, at):
     lanes = own_ref.shape[2]
     first = iota((at.size, lanes), 1) < lanes // 2
-    ins, cots = [], []
-    for ref in (own_ref, oth_ref):
-        even, odd = ref[0, at, :], ref[1, at, :]
-        ins.append(jnp.where(first, even, odd))
-        cots.append(jnp.where(first, odd, even))
-    return jnp.concatenate(ins, axis=1), jnp.concatenate(cots, axis=1)
-
-
-def turn(value, lanes):
-    blocks = [
-        pltpu.roll(value[:, at : at + lanes], lanes // 2, 1)
-        for at in range(0, value.shape[1], lanes)
-    ]
-    return jnp.concatenate(blocks, axis=1)
+    even, odd = own_ref[0, at, :], own_ref[1, at, :]
+    return jnp.where(first, even, odd), jnp.where(first, odd, even)
+
+
+def turn(value):
+    return pltpu.roll(value, value.shape[1] // 2, 1)
 
 
 def expert_kernel(
-    own_ref, oth_ref, wg_ref, wu_ref, wd_ref, keep_ref, send_ref, cots_ref, act_ref
+    own_ref, wg_ref, wu_ref, wd_ref, hg_ref, hu_ref, hd_ref, back_ref, cots_ref, act_ref
 ):
     dim, lanes = own_ref.shape[1:]
     units = wg_ref.shape[0]
-    width = keep_ref.shape[2] * 2
-
-    def two(at):
-        return jnp.concatenate([wg_ref[:, at], wu_ref[:, at]], axis=0)
-
-    fwd = jnp.zeros((2 * units, 2 * lanes), F32)
-    grad_act = jnp.zeros((units, 2 * lanes), F32)
+    width = back_ref.shape[1] * 2
+
+    def both(at):
+        return jnp.concatenate(
+            [wg_ref[:, at], hg_ref[:, at], wu_ref[:, at], hu_ref[:, at]], axis=0
+        )
+
+    fwd = jnp.zeros((4 * units, lanes), F32)
+    grad_act = jnp.zeros((2 * units, lanes), F32)
     for i in range(dim // STEP):
         at = pl.ds(i * STEP, STEP)
-        rows_in, rows_grad = rows_at(own_ref, oth_ref, at)
-        fwd = fwd + jnp.dot(two(at), rows_in, preferred_element_type=F32)
-        grad_act = grad_act + jnp.dot(wd_ref[:, at], rows_grad, preferred_element_type=F32)
-    grad_act = turn(grad_act, lanes)
-    pre_act, up_value = fwd[:units], fwd[units:]
+        rows_in, rows_grad = rows_at(own_ref, at)
+        down = jnp.concatenate([wd_ref[:, at], hd_ref[:, at]], axis=0)
+        fwd = fwd + jnp.dot(both(at), rows_in, preferred_element_type=F32)
+        grad_act = grad_act + jnp.dot(down, rows_grad, preferred_element_type=F32)
+    grad_act = turn(grad_act)
+    pre_act, up_value = fwd[: 2 * units], fwd[2 * units :]
     sig = jax.nn.sigmoid(pre_act)
     silu = pre_act * sig
     slope = sig * (1.0 + pre_act * (1.0 - sig))
-    act_ref[...] = turn(silu * up_value, lanes).astype(BF16)
+    act_ref[...] = turn(silu * up_value).astype(BF16)
     grad_pre = (grad_act * up_value * slope).astype(BF16)
     grad_upv = (grad_act * silu).astype(BF16)
     cots = jnp.concatenate([grad_pre, grad_upv], axis=0)
@@ -172,62 +167,58 @@
     first = iota((width // 2, lanes), 1) < lanes // 2
     for i in range(dim // STEP):
         at = pl.ds(i * STEP, STEP)
-        total = lax.dot_general(two(at), cots, FIRST, preferred_element_type=F32)
+        total = lax.dot_general(both(at), cots, FIRST, preferred_element_type=F32)
         for j in range(STEP // width):
             e = i * (STEP // width) + j
-            for ref, begin in ((keep_ref, 0), (send_ref, lanes)):
-                block = total[j * width : (j + 1) * width, begin : begin + lanes]
-                upper, lower = block[: width // 2], block[width // 2 :]
-                even = jnp.where(first, upper, pltpu.roll(lower, lanes // 2, 1))
-                odd = jnp.where(first, pltpu.roll(upper, lanes // 2, 1), lower)
-                ref[0, e] = even.astype(ref.dtype)
-                ref[1, e] = odd.astype(ref.dtype)
-
-
-def expert(own, oth, w_gate, w_up, w_down, width):
-    units, dim = w_gate.shape
+            upper = total[j * width : j * width + width // 2]
+            lower = total[j * width + width // 2 : (j + 1) * width]
+            back_ref[e] = jnp.where(first, upper, turn(lower)).astype(BF16)
+            back_ref[EXPERTS + e] = jnp.where(first, turn(upper), lower).astype(BF16)
+
+
+def expert(own, mine, other, width):
+    units, dim = mine[0].shape
     lanes = own.shape[2]
-    back = (PAIR, EXPERTS, width // 2, lanes)
     return pl.pallas_call(
         expert_kernel,
         out_shape=(
-            jax.ShapeDtypeStruct(back, F32),
-            jax.ShapeDtypeStruct(back, BF16),
-            jax.ShapeDtypeStruct((2 * units, 2 * lanes), BF16),
-            jax.ShapeDtypeStruct((units, 2 * lanes), BF16),
+            jax.ShapeDtypeStruct((PAIR * EXPERTS, width // 2, lanes), BF16),
+            jax.ShapeDtypeStruct((4 * units, lanes), BF16),
+            jax.ShapeDtypeStruct((2 * units, lanes), BF16),
         ),
         cost_estimate=pl.CostEstimate(
-            flops=2 * 5 * units * dim * 2 * lanes, bytes_accessed=9 << 20, transcendentals=0
+            flops=2 * 10 * units * dim * lanes, bytes_accessed=6 << 20, transcendentals=0
         ),
         compiler_params=pltpu.CompilerParams(vmem_limit_bytes=VMEM_BYTES),
-    )(own, oth, w_gate, w_up, w_down)
-
-
-def grads_kernel(own_ref, oth_ref, cots_ref, act_ref, gg_ref, gu_ref, gd_ref):
+    )(own, *mine, *other)
+
+
+def grads_kernel(own_ref, cots_ref, act_ref, gg_ref, gu_ref, gd_ref, send_ref):
     units, dim = gg_ref.shape
     for i in range(dim // STEP):
         at = pl.ds(i * STEP, STEP)
-        rows_in, rows_grad = rows_at(own_ref, oth_ref, at)
+        rows_in, rows_grad = rows_at(own_ref, at)
         grads = lax.dot_general(cots_ref[...], rows_in, LAST, preferred_element_type=F32)
-        grads = grads.astype(BF16)
+        down = lax.dot_general(act_ref[...], rows_grad, LAST, preferred_element_type=F32)
         gg_ref[:, at] = grads[:units]
-        gu_ref[:, at] = grads[units:]
-        gd_ref[:, at] = lax.dot_general(
-            act_ref[...], rows_grad, LAST, preferred_element_type=F32
-        ).astype(BF16)
-
-
-def weight_grads(own, oth, cots, act):
-    units, dim = act.shape[0], own.shape[1]
-    grad = jax.ShapeDtypeStruct((units, dim), BF16)
+        gu_ref[:, at] = grads[2 * units : 3 * units]
+        gd_ref[:, at] = down[:units]
+        send_ref[0, :, at] = grads[units : 2 * units].astype(BF16)
+        send_ref[1, :, at] = grads[3 * units :].astype(BF16)
+        send_ref[2, :, at] = down[units:].astype(BF16)
+
+
+def weight_grads(own, cots, act):
+    units, dim = act.shape[0] // 2, own.shape[1]
+    grad = jax.ShapeDtypeStruct((units, dim), F32)
     return pl.pallas_call(
         grads_kernel,
-        out_shape=(grad, grad, grad),
+        out_shape=(grad, grad, grad, jax.ShapeDtypeStruct((3, units, dim), BF16)),
         cost_estimate=pl.CostEstimate(
-            flops=2 * 3 * units * dim * act.shape[1], bytes_accessed=5 << 20, transcendentals=0
+            flops=2 * 6 * units * dim * act.shape[1], bytes_accessed=7 << 20, transcendentals=0
         ),
         compiler_params=pltpu.CompilerParams(vmem_limit_bytes=VMEM_BYTES),
-    )(own, oth, cots, act)
+    )(own, cots, act)
 
 
 def combine_kernel(back_ref, table_ref, out_ref):
@@ -268,44 +259,38 @@
     )(back, table)
 
 
-def sum_kernel(parts_ref, out_ref):
-    total = parts_ref[0].astype(F32)
-    for i in range(1, parts_ref.shape[0]):
-        total = total + parts_ref[i].astype(F32)
-    out_ref[...] = total[:, : out_ref.shape[1]].astype(BF16)
-
-
-def add_parts(parts, width):
-    return pl.pallas_call(
-        sum_kernel, out_shape=jax.ShapeDtypeStruct((parts.shape[1], width), BF16)
-    )(parts)
-
-
-def exchange(value, axis):
-    return lax.all_to_all(value, axis, split_axis=0, concat_axis=0, tiled=True)
+def exchange(value, axis, groups=None):
+    return lax.all_to_all(
+        value, axis, split_axis=0, concat_axis=0, tiled=True, axis_index_groups=groups
+    )
 
 
 SWAP = [(0, 1), (1, 0)]
 WIDE = ("pair", "y", "x")
+
+
+def along_z():
+    return [[(FAR // 2 + i) % FAR * PAIR + p for i in range(FAR)] for p in range(PAIR)]
 
 
 def shards(tokens, grad_out, routes, gate_probs, w_gate, w_up, w_down):
     tok_rows, width = tokens.shape
     dim = w_gate.shape[2]
-    w_gate, w_up, w_down = w_gate[0], w_up[0], w_down[0]
+    mine = (w_gate[0], w_up[0], w_down[0])
+    other = tuple(lax.ppermute(w, "core", SWAP) for w in mine)
     pair = lax.axis_index("pair").astype(jnp.int32).reshape(1)
-    far = exchange(message(tokens, grad_out, routes, gate_probs), "far")
+    far = exchange(message(tokens, grad_out, routes, gate_probs), ("far", "pair"), along_z())
     slots, table = pack(pair, far.reshape(FAR * tok_rows, ROW), width)
     own = exchange(slots, WIDE).reshape(PAIR, dim, -1)
-    oth = lax.ppermute(own, "core", SWAP)
-    keep, send, cots, act = expert(own, oth, w_gate, w_up, w_down, width)
-    back = (keep + lax.ppermute(send, "core", SWAP).astype(F32)).astype(BF16)
-    back = exchange(back.reshape((PAIR * EXPERTS,) + back.shape[2:]), WIDE)
-    part = combine(back, table)
-    part = exchange(part.reshape(FAR, tok_rows, part.shape[1]), "far")
-    grad_in = add_parts(part, width)
-    grad_gate, grad_up, grad_down = weight_grads(own, oth, cots, act)
-    return grad_in, grad_gate[None], grad_up[None], grad_down[None]
+    back, cots, act = expert(own, mine, other, width)
+    part = combine(exchange(back, WIDE), table)
+    part = exchange(part.reshape(FAR, tok_rows, part.shape[1]), ("far", "pair"), along_z())
+    part = lax.optimization_barrier(part.astype(F32))
+    grad_in = part.sum(axis=0)[:, :width].astype(BF16)
+    *halves, send = weight_grads(own, cots, act)
+    send = lax.ppermute(send, "core", SWAP)
+    grads = [(half + send[i].astype(F32)).astype(BF16)[None] for i, half in enumerate(halves)]
+    return grad_in, *grads
 
 
 def solution(mesh):

time: 151 us -> 137 us (0.907)
  blocking collectives: 40.2 us -> 0 us
  starting transfers between devices: 51.6 us -> 81.7 us
  waiting for transfers between devices: 46.7 us -> 26.9 us
  local copies, waits for them, and re-layouts: 0.65 us -> 10.7 us
  other arithmetic: 0.18 us -> 4.2 us
    all_to_all x2 -> x0, blocking collectives: 40.2 us -> none  [exchange(): return lax.all_to_all(value, axis, split_axis=0, concat_axis=0, tiled=True)]
    all_to_all x2 -> x4, starting transfers between devices: 40.8 us -> 71.4 us  [exchange(): lax.all_to_all(value, axis, split_axis=0, concat_axis=0, tiled=True, axis...]
    all_to_all x2 -> x4, waiting for transfers between devices: 41.8 us -> 26.9 us  [exchange(): lax.all_to_all(value, axis, split_axis=0, concat_axis=0, tiled=True, axis...]
    unnamed x8 -> x30, local copies, waits for them, and re-layouts: 0.65 us -> 10.7 us
    ppermute x2 -> x4, waiting for transfers between devices: 4.9 us -> 0.01 us  [the longest x3 0.01 us: shards(): other = tuple((lax.ppermute(w, 'core', SWAP) for w in mine))]
    broadcast_in_dim x0 -> x1, other arithmetic: none -> 3.58 us  [shards(): (half + send[i].astype(F32)).astype(BF16)[None]]
    ppermute x2 -> x4, starting transfers between devices: 10.7 us -> 10.3 us  [the longest x3 7.37 us: shards(): other = tuple((lax.ppermute(w, 'core', SWAP) for w in mine))]
    pallas_call x3 -> x2, Pallas kernels: 5.82 us -> 5.44 us  [the longest x1 3.06 us: expert(): pl.pallas_call(expert_kernel, out_shape=(jax.ShapeDtypeStruct((PAIR * EXP...]
  transfers between devices with their start and end apart: 4 -> 8, of which waited for: 4 -> 4; matrix products, arithmetic and copies ran while one was open for 0% -> 3% of each run, Pallas kernels for 2% -> 3%
where the time goes in v3:
time: 137 us; the launch traced here: 134 us
  starting transfers between devices  81.7 us (60%)
  waiting for transfers between devices  26.9 us (20%)
  local copies, waits for them, and re-layouts  10.7 us (8%)
  Pallas kernels  9.87 us (7%)
  other arithmetic  4.2 us (3%)
    all_to_all x4, starting transfers between devices, exchange(): lax.all_to_all(value, axis, split_axis=0, concat_axis=0, tiled=True, axis...  71.4 us
    all_to_all x4, waiting for transfers between devices, exchange(): lax.all_to_all(value, axis, split_axis=0, concat_axis=0, tiled=True, axis...  26.9 us
    unnamed x30, local copies, waits for them, and re-layouts  10.7 us
    ppermute x3, starting transfers between devices, shards(): other = tuple((lax.ppermute(w, 'core', SWAP) for w in mine))  7.37 us
    broadcast_in_dim x1, other arithmetic, shards(): (half + send[i].astype(F32)).astype(BF16)[None]  3.58 us
    pallas_call x1, Pallas kernels, expert(): pl.pallas_call(expert_kernel, out_shape=(jax.ShapeDtypeStruct((PAIR * EXP...  3.06 us
    ppermute x1, starting transfers between devices, shards(): send = lax.ppermute(send, 'core', SWAP)  2.97 us
  transfers between devices with their start and end apart: 8, of which 4 were waited for; matrix products, arithmetic and copies ran while one was open for 3% of the time, Pallas kernels for 3%

profile of v3, /device:TPU:1, one launch (start us, length us, event | category | flops | bytes accessed | tf_op | source)
XLA Modules:
  0.0 134.1 jit_solution(13314172390859115930)
XLA Ops:
  0.6 1.5 %shard_map.102 = bf16[16,8,512]{2,1,0:T(8,128)(2,1)} custom-call(bf16[8,192]{1,0:T(8,128)(2,1)} %tokens_ref.1, bf16[8,192]{1,0:T(8,128)(2,1)} %grad_ref.1, s32[4,8]{1,0:T(4,128)} %bitcast.41, f32[4,8]{1,0:T(4,128)} %bitcast.42), custom_call_target="tpu_custom_call" | custom-call | tf_op jit(solution)/shard_map/pallas_call | solution.py:64
  2.1 35.6 %all-to-all-start = ((bf16[16,8,512]{2,1,0:T(8,128)(2,1)}), bf16[16,8,512]{2,1,0:T(8,128)(2,1)S(1)}, u32[]{:S(2)}, u32[]{:S(2)}) async-start(bf16[16,8,512]{2,1,0:T(8,128)(2,1)} %shard_map.102), calls=%async_computation | async-start | bytes 262144 | tf_op jit(solution)/shard_map/all_to_all | solution.py:263
  37.7 12.6 %all-to-all-done = bf16[16,8,512]{2,1,0:T(8,128)(2,1)S(1)} async-done(((bf16[16,8,512]{2,1,0:T(8,128)(2,1)}), bf16[16,8,512]{2,1,0:T(8,128)(2,1)S(1)}, u32[]{:S(2)}, u32[]{:S(2)}) %all-to-all-start) | async-done | bytes 131104 | tf_op jit(solution)/shard_map/all_to_all | solution.py:263
  50.3 1.8 %shard_map.103 = (bf16[32,192,128]{2,1,0:T(8,128)(2,1)}, f32[16,128]{1,0:T(8,128)S(1)}) custom-call(s32[1]{0:T(128)} %bitcast.pair_ref, bf16[128,512]{1,0:T(8,128)(2,1)S(1)} %bitcast.39), custom_call_target="tpu_custom_call" | custom-call | tf_op jit(solution)/shard_map/pallas_call | solution.py:112
  52.1 7.5 %all-to-all-start.1 = ((bf16[32,192,128]{2,1,0:T(8,128)(2,1)}), bf16[32,192,128]{2,1,0:T(8,128)(2,1)S(1)}, u32[]{:S(2)}, u32[]{:S(2)}) async-start(bf16[32,192,128]{2,1,0:T(8,128)(2,1)} %get-tuple-element.13), calls=%async_computation.1 | async-start | bytes 3145728 | tf_op jit(solution)/shard_map/all_to_all | solution.py:263
  59.6 3.0 %collective-permute-start = (bf16[96,3072]{1,0:T(8,128)(2,1)S(1)}, bf16[96,3072]{1,0:T(8,128)(2,1)S(1)}, u32[]{:S(2)}, u32[]{:S(2)}) collective-permute-start(bf16[96,3072]{1,0:T(8,128)(2,1)S(1)} %bitcast.33), channel_id=1, source_target_pairs={{0,16},{16,0},{1,17},{17,1},{2,18},{18,2},{3,19},{19,3},{4,20},{20... | collective-permute-start | bytes 1769480 | tf_op jit(solution)/shard_map/ppermute | solution.py:280
  62.7 1.9 %collective-permute-start.1 = (bf16[96,3072]{1,0:T(8,128)(2,1)S(1)}, bf16[96,3072]{1,0:T(8,128)(2,1)S(1)}, u32[]{:S(2)}, u32[]{:S(2)}) collective-permute-start(bf16[96,3072]{1,0:T(8,128)(2,1)S(1)} %bitcast.35), channel_id=1, source_target_pairs={{0,16},{16,0},{1,17},{17,1},{2,18},{18,2},{3,19},{19,3},{4,20},{20... | collective-permute-start | bytes 1769480 | tf_op jit(solution)/shard_map/ppermute | solution.py:280
  64.7 2.4 %collective-permute-start.2 = (bf16[96,3072]{1,0:T(8,128)(2,1)S(1)}, bf16[96,3072]{1,0:T(8,128)(2,1)S(1)}, u32[]{:S(2)}, u32[]{:S(2)}) collective-permute-start(bf16[96,3072]{1,0:T(8,128)(2,1)S(1)} %bitcast.37), channel_id=1, source_target_pairs={{0,16},{16,0},{1,17},{17,1},{2,18},{18,2},{3,19},{19,3},{4,20},{20... | collective-permute-start | bytes 1769480 | tf_op jit(solution)/shard_map/ppermute | solution.py:280
  69.5 10.2 %all-to-all-done.1 = bf16[32,192,128]{2,1,0:T(8,128)(2,1)S(1)} async-done(((bf16[32,192,128]{2,1,0:T(8,128)(2,1)}), bf16[32,192,128]{2,1,0:T(8,128)(2,1)S(1)}, u32[]{:S(2)}, u32[]{:S(2)}) %all-to-all-start.1) | async-done | bytes 1572896 | tf_op jit(solution)/shard_map/all_to_all | solution.py:263
  79.7 1.1 copy-done.6
  80.8 1.1 copy-done.8
  81.9 1.1 copy-done.10
  82.9 3.1 %shard_map.104 = (bf16[32,96,128]{2,1,0:T(8,128)(2,1)}, bf16[384,128]{1,0:T(8,128)(2,1)S(1)}, bf16[192,128]{1,0:T(8,128)(2,1)S(1)}) custom-call(bf16[2,3072,128]{2,1,0:T(8,128)(2,1)S(1)} %bitcast.31, bf16[96,3072]{1,0:T(8,128)(2,1)S(1)} %bitcast.34, bf16[96,3072]{1,0:T(8,128)(2,1)S(1)} %bitcast.36, bf16[96,3072]{1,0:T(8,128)(2,1)S(1)} %bitcast.38, ...), custom_call_target="tpu_custom_call" | custom-call | flops 754974720 | bytes 6291456 | tf_op jit(solution)/shard_map/pallas_call | solution.py:182
  87.3 7.3 %all-to-all-start.2 = ((bf16[32,96,128]{2,1,0:T(8,128)(2,1)}), bf16[32,96,128]{2,1,0:T(8,128)(2,1)S(1)}, u32[]{:S(2)}, u32[]{:S(2)}) async-start(bf16[32,96,128]{2,1,0:T(8,128)(2,1)} %get-tuple-element.14), calls=%async_computation.2 | async-start | bytes 1572864 | tf_op jit(solution)/shard_map/all_to_all | solution.py:263
  94.5 0.9 copy-done.12
  96.2 2.4 %shard_map.106 = (f32[96,3072]{1,0:T(8,128)S(1)}, f32[96,3072]{1,0:T(8,128)S(1)}, f32[96,3072]{1,0:T(8,128)S(1)}, bf16[3,96,3072]{2,1,0:T(8,128)(2,1)}) custom-call(bf16[2,3072,128]{2,1,0:T(8,128)(2,1)S(1)} %bitcast.32, bf16[384,128]{1,0:T(8,128)(2,1)S(1)} %copy-done.12, bf16[192,128]{1,0:T(8,128)(2,1)S(1)} %copy-done.14), custom_call_target="tpu_custom_call" | custom-call | flops 452984832 | bytes 7340032 | tf_op jit(solution)/shard_map/pallas_call | solution.py:214
  98.6 1.1 copy-done
  99.7 1.0 copy-done.1
  100.7 3.0 %collective-permute-start.3 = (bf16[3,96,3072]{2,1,0:T(8,128)(2,1)}, bf16[3,96,3072]{2,1,0:T(8,128)(2,1)}, u32[]{:S(2)}, u32[]{:S(2)}) collective-permute-start(bf16[3,96,3072]{2,1,0:T(8,128)(2,1)} %get-tuple-element.19), channel_id=1, source_target_pairs={{0,16},{16,0},{1,17},{17,1},{2,18},{18,2},{3,19},{19,3},{4,20},{20... | collective-permute-start | bytes 5308424 | tf_op jit(solution)/shard_map/ppermute | solution.py:291
  103.7 3.1 %all-to-all-done.2.back_ref = bf16[32,96,128]{2,1,0:T(8,128)(2,1)S(1)} async-done(((bf16[32,96,128]{2,1,0:T(8,128)(2,1)}), bf16[32,96,128]{2,1,0:T(8,128)(2,1)S(1)}, u32[]{:S(2)}, u32[]{:S(2)}) %all-to-all-start.2) | async-done | bytes 786464 | tf_op jit(solution)/shard_map/all_to_all | solution.py:263
  106.8 1.1 shard_map.105
  107.9 21.1 %all-to-all-start.3 = ((bf16[16,8,256]{2,1,0:T(8,128)(2,1)}), bf16[16,8,256]{2,1,0:T(8,128)(2,1)S(1)}, u32[]{:S(2)}, u32[]{:S(2)}) async-start(bf16[16,8,256]{2,1,0:T(8,128)(2,1)} %bitcast.8), calls=%async_computation.3 | async-start | bytes 131072 | tf_op jit(solution)/shard_map/all_to_all | solution.py:263
  129.0 3.6 %fusion.5 = (bf16[1,96,3072]{2,1,0:T(8,128)(2,1)}, bf16[1,96,3072]{2,1,0:T(8,128)(2,1)}, bf16[1,96,3072]{2,1,0:T(8,128)(2,1)}) fusion(f32[96,3072]{1,0:T(8,128)} %copy-done.1, bf16[3,96,3072]{2,1,0:T(8,128)(2,1)} %collective-permute-done.3, f32[96,3072]{1,0:T(8,128)} %copy-done, f32[96,3072]{1,0:T(8,128)S(1)} %get-tuple-element.18), kind=kLoop, calls=%fused_computation.8 | loop fusion | flops 2654208 | bytes 7077888 | tf_op jit(solution)/shard_map/broadcast_in_dim | solution.py:292
  132.5 1.0 all-to-all-done.3
  (30 shorter events, 5.2 us)
Async XLA Ops:
  2.1 48.2 %all-to-all-start = ((bf16[16,8,512]{2,1,0:T(8,128)(2,1)}), bf16[16,8,512]{2,1,0:T(8,128)(2,1)S(1)}, u32[]{:S(2)}, u32[]{:S(2)}) async-start(bf16[16,8,512]{2,1,0:T(8,128)(2,1)} %shard_map.102), calls=%async_computation | async-start | bytes 262144 | tf_op jit(solution)/shard_map/all_to_all | solution.py:263
  52.1 7.5 %copy-start.2 = (bf16[1,96,3072]{2,1,0:T(8,128)(2,1)S(1)}, bf16[1,96,3072]{2,1,0:T(8,128)(2,1)}, u32[]{:S(2)}) copy-start(bf16[1,96,3072]{2,1,0:T(8,128)(2,1)} %param.11) | copy-start | bytes 1769476
  52.1 10.6 %copy-start.3 = (bf16[1,96,3072]{2,1,0:T(8,128)(2,1)S(1)}, bf16[1,96,3072]{2,1,0:T(8,128)(2,1)}, u32[]{:S(2)}) copy-start(bf16[1,96,3072]{2,1,0:T(8,128)(2,1)} %param.12) | copy-start | bytes 1769476
  52.1 12.5 %copy-start.4 = (bf16[1,96,3072]{2,1,0:T(8,128)(2,1)S(1)}, bf16[1,96,3072]{2,1,0:T(8,128)(2,1)}, u32[]{:S(2)}) copy-start(bf16[1,96,3072]{2,1,0:T(8,128)(2,1)} %param.13) | copy-start | bytes 1769476
  52.1 27.6 %all-to-all-start.1 = ((bf16[32,192,128]{2,1,0:T(8,128)(2,1)}), bf16[32,192,128]{2,1,0:T(8,128)(2,1)S(1)}, u32[]{:S(2)}, u32[]{:S(2)}) async-start(bf16[32,192,128]{2,1,0:T(8,128)(2,1)} %get-tuple-element.13), calls=%async_computation.1 | async-start | bytes 3145728 | tf_op jit(solution)/shard_map/all_to_all | solution.py:263
  59.6 7.4 %collective-permute-start = (bf16[96,3072]{1,0:T(8,128)(2,1)S(1)}, bf16[96,3072]{1,0:T(8,128)(2,1)S(1)}, u32[]{:S(2)}, u32[]{:S(2)}) collective-permute-start(bf16[96,3072]{1,0:T(8,128)(2,1)S(1)} %bitcast.33), channel_id=1, source_target_pairs={{0,16},{16,0},{1,17},{17,1},{2,18},{18,2},{3,19},{19,3},{4,20},{20... | collective-permute-start | bytes 1769480 | tf_op jit(solution)/shard_map/ppermute | solution.py:280
  62.7 5.2 %collective-permute-start.1 = (bf16[96,3072]{1,0:T(8,128)(2,1)S(1)}, bf16[96,3072]{1,0:T(8,128)(2,1)S(1)}, u32[]{:S(2)}, u32[]{:S(2)}) collective-permute-start(bf16[96,3072]{1,0:T(8,128)(2,1)S(1)} %bitcast.35), channel_id=1, source_target_pairs={{0,16},{16,0},{1,17},{17,1},{2,18},{18,2},{3,19},{19,3},{4,20},{20... | collective-permute-start | bytes 1769480 | tf_op jit(solution)/shard_map/ppermute | solution.py:280
  64.7 4.1 %collective-permute-start.2 = (bf16[96,3072]{1,0:T(8,128)(2,1)S(1)}, bf16[96,3072]{1,0:T(8,128)(2,1)S(1)}, u32[]{:S(2)}, u32[]{:S(2)}) collective-permute-start(bf16[96,3072]{1,0:T(8,128)(2,1)S(1)} %bitcast.37), channel_id=1, source_target_pairs={{0,16},{16,0},{1,17},{17,1},{2,18},{18,2},{3,19},{19,3},{4,20},{20... | collective-permute-start | bytes 1769480 | tf_op jit(solution)/shard_map/ppermute | solution.py:280
  67.1 0.8 copy-start.5
  67.9 0.8 copy-start.7
  68.7 0.8 copy-start.9
  79.7 1.1 copy-start.6
  80.8 1.1 copy-start.8
  81.9 1.1 copy-start.10
  86.0 0.6 copy-start.11
  86.6 0.6 copy-start.13
  87.3 19.5 %all-to-all-start.2 = ((bf16[32,96,128]{2,1,0:T(8,128)(2,1)}), bf16[32,96,128]{2,1,0:T(8,128)(2,1)S(1)}, u32[]{:S(2)}, u32[]{:S(2)}) async-start(bf16[32,96,128]{2,1,0:T(8,128)(2,1)} %get-tuple-element.14), calls=%async_computation.2 | async-start | bytes 1572864 | tf_op jit(solution)/shard_map/all_to_all | solution.py:263
  94.5 0.9 copy-start.12
  95.4 0.8 copy-start.14
  98.6 1.1 copy-start
  99.7 1.0 copy-start.1
  100.7 28.3 %collective-permute-start.3 = (bf16[3,96,3072]{2,1,0:T(8,128)(2,1)}, bf16[3,96,3072]{2,1,0:T(8,128)(2,1)}, u32[]{:S(2)}, u32[]{:S(2)}) collective-permute-start(bf16[3,96,3072]{2,1,0:T(8,128)(2,1)} %get-tuple-element.19), channel_id=1, source_target_pairs={{0,16},{16,0},{1,17},{17,1},{2,18},{18,2},{3,19},{19,3},{4,20},{20... | collective-permute-start | bytes 5308424 | tf_op jit(solution)/shard_map/ppermute | solution.py:291
  107.9 25.6 %all-to-all-start.3 = ((bf16[16,8,256]{2,1,0:T(8,128)(2,1)}), bf16[16,8,256]{2,1,0:T(8,128)(2,1)S(1)}, u32[]{:S(2)}, u32[]{:S(2)}) async-start(bf16[16,8,256]{2,1,0:T(8,128)(2,1)} %bitcast.8), calls=%async_computation.3 | async-start | bytes 131072 | tf_op jit(solution)/shard_map/all_to_all | solution.py:263

commit v4 on v3

--- a/solution.py
+++ b/solution.py
@@ -15,9 +15,7 @@
 VMEM_BYTES = 24 * 1024 * 1024
 LAST = (((1,), (1,)), ((), ()))
 FIRST = (((0,), (0,)), ((), ()))
-GRAD_AT = 256
-ROW = 512
-STEP = 384
+STEP = 768
 
 
 def iota(shape, dim):
@@ -51,29 +49,41 @@
         piece = rest.astype(BF16).astype(F32)
         meta = jnp.where(kind == 5 + part, piece, meta)
         rest = rest - piece
-    meta = meta.astype(BF16)
-    blank = jnp.zeros((tok_rows, 128), BF16)
+    half = tok_rows // 2
+    tokens, grad = tokens_ref[...].astype(F32), grad_ref[...].astype(F32)
+    pad = jnp.zeros((tok_rows, 256 - width), F32)
+    tokens = jnp.concatenate([tokens, pad], axis=1)
+    grad = jnp.concatenate([grad, pad], axis=1)
+    blocks = []
+    for chunk in (tokens[:, :128], tokens[:, 128:] + meta, grad[:, :128]):
+        blocks += [chunk[:half], chunk[half:]]
+    blocks.append(grad[:half, 128:] + pltpu.roll(grad[:, 128:], 64, 1)[half:])
+    blocks = [block.astype(BF16) for block in blocks]
     for copy in range(out_ref.shape[0]):
-        out_ref[copy, :, 128:256] = meta
-        out_ref[copy, :, 0:width] = tokens_ref[...]
-        out_ref[copy, :, GRAD_AT + 128 : ROW] = blank
-        out_ref[copy, :, GRAD_AT : GRAD_AT + width] = grad_ref[...]
+        for i, block in enumerate(blocks):
+            out_ref[copy, i] = block
 
 
 def message(tokens, grad_out, routes, probs):
     return pl.pallas_call(
         message_kernel,
-        out_shape=jax.ShapeDtypeStruct((FAR, tokens.shape[0], ROW), BF16),
+        out_shape=jax.ShapeDtypeStruct((FAR, 7, tokens.shape[0] // 2, 128), BF16),
     )(tokens, grad_out, routes.T, probs.T)
 
 
 def pack_kernel(pair_ref, msg_ref, out_ref, table_ref):
-    toks = msg_ref.shape[0]
+    toks = table_ref.shape[1]
     width, lanes = out_ref.shape[1:]
     half = lanes // 2
-    left = msg_ref[:, 0:GRAD_AT].astype(F32)
+
+    def chunk(i):
+        return msg_ref[:, 2 * i : 2 * i + 2].astype(F32).reshape(toks, 128)
+
+    last = msg_ref[:, 6].astype(F32)
+    last = jnp.stack([last, pltpu.roll(last, 64, 2)], axis=1).reshape(toks, 128)
+    left = jnp.concatenate([chunk(0), chunk(1)], axis=1)
     left_t = jnp.transpose(left)
-    right_t = jnp.transpose(msg_ref[:, GRAD_AT:ROW].astype(F32))
+    right_t = jnp.transpose(jnp.concatenate([chunk(2), last], axis=1))
     table_ref[...] = left_t[width : width + EXPERTS]
     top = jnp.concatenate([left_t[:width], right_t[:width]], axis=1)
     parts = left_t[width + EXPERTS : width + 4 * EXPERTS]
@@ -108,7 +118,7 @@
 
 
 def pack(pair, msgs, width):
-    toks = msgs.shape[0]
+    toks = msgs.shape[0] * msgs.shape[2] * 2
     return pl.pallas_call(
         pack_kernel,
         in_specs=[
@@ -135,7 +145,8 @@
 
 
 def expert_kernel(
-    own_ref, wg_ref, wu_ref, wd_ref, hg_ref, hu_ref, hd_ref, back_ref, cots_ref, act_ref
+    own_ref, wg_ref, wu_ref, wd_ref, hg_ref, hu_ref, hd_ref, back_ref, cots_ref,
+    total_ref, sems,
 ):
     dim, lanes = own_ref.shape[1:]
     units = wg_ref.shape[0]
@@ -159,33 +170,53 @@
     sig = jax.nn.sigmoid(pre_act)
     silu = pre_act * sig
     slope = sig * (1.0 + pre_act * (1.0 - sig))
-    act_ref[...] = turn(silu * up_value).astype(BF16)
     grad_pre = (grad_act * up_value * slope).astype(BF16)
     grad_upv = (grad_act * silu).astype(BF16)
     cots = jnp.concatenate([grad_pre, grad_upv], axis=0)
-    cots_ref[...] = cots
+    cots_ref[: 4 * units] = cots
+    cots_ref[4 * units :] = turn(silu * up_value).astype(BF16)
+    wide = jnp.concatenate([cots, turn(cots)], axis=1)
     first = iota((width // 2, lanes), 1) < lanes // 2
+    per = STEP // width
+    stores = []
     for i in range(dim // STEP):
         at = pl.ds(i * STEP, STEP)
-        total = lax.dot_general(both(at), cots, FIRST, preferred_element_type=F32)
-        for j in range(STEP // width):
-            e = i * (STEP // width) + j
+        total = lax.dot_general(both(at), wide, FIRST, preferred_element_type=F32)
+        for j in range(per):
+            e = i * per + j
             upper = total[j * width : j * width + width // 2]
             lower = total[j * width + width // 2 : (j + 1) * width]
-            back_ref[e] = jnp.where(first, upper, turn(lower)).astype(BF16)
-            back_ref[EXPERTS + e] = jnp.where(first, turn(upper), lower).astype(BF16)
+            even = jnp.where(first, upper[:, :lanes], lower[:, lanes:])
+            odd = jnp.where(first, upper[:, lanes:], lower[:, :lanes])
+            total_ref[e] = even.astype(BF16)
+            total_ref[EXPERTS + e] = odd.astype(BF16)
+        for p in range(PAIR):
+            part = pl.ds(p * EXPERTS + i * per, per)
+            copy = pltpu.make_async_copy(total_ref.at[part], back_ref.at[part], sems.at[i, p])
+            copy.start()
+            stores.append(copy)
+    for copy in stores:
+        copy.wait()
 
 
 def expert(own, mine, other, width):
     units, dim = mine[0].shape
     lanes = own.shape[2]
+    back = (PAIR * EXPERTS, width // 2, lanes)
     return pl.pallas_call(
         expert_kernel,
         out_shape=(
-            jax.ShapeDtypeStruct((PAIR * EXPERTS, width // 2, lanes), BF16),
-            jax.ShapeDtypeStruct((4 * units, lanes), BF16),
-            jax.ShapeDtypeStruct((2 * units, lanes), BF16),
-        ),
+            pltpu.HBM(back, BF16),
+            jax.ShapeDtypeStruct((6 * units, lanes), BF16),
+        ),
+        out_specs=(
+            pl.BlockSpec(memory_space=pltpu.HBM),
+            pl.BlockSpec(memory_space=pltpu.VMEM),
+        ),
+        scratch_shapes=[
+            pltpu.VMEM(back, BF16),
+            pltpu.SemaphoreType.DMA((dim // STEP, PAIR)),
+        ],
         cost_estimate=pl.CostEstimate(
             flops=2 * 10 * units * dim * lanes, bytes_accessed=6 << 20, transcendentals=0
         ),
@@ -193,32 +224,62 @@
     )(own, *mine, *other)
 
 
-def grads_kernel(own_ref, cots_ref, act_ref, gg_ref, gu_ref, gd_ref, send_ref):
+def grads_kernel(
+    own_ref, cots_ref, gg_ref, gu_ref, gd_ref, send_ref, half_ref, keep_ref, give_ref, sems
+):
     units, dim = gg_ref.shape
-    for i in range(dim // STEP):
+    steps = dim // STEP
+    load = pltpu.make_async_copy(cots_ref, half_ref, sems.at[steps, 0])
+    load.start()
+    load.wait()
+    stores = []
+    for i in range(steps):
         at = pl.ds(i * STEP, STEP)
         rows_in, rows_grad = rows_at(own_ref, at)
-        grads = lax.dot_general(cots_ref[...], rows_in, LAST, preferred_element_type=F32)
-        down = lax.dot_general(act_ref[...], rows_grad, LAST, preferred_element_type=F32)
-        gg_ref[:, at] = grads[:units]
-        gu_ref[:, at] = grads[2 * units : 3 * units]
-        gd_ref[:, at] = down[:units]
-        send_ref[0, :, at] = grads[units : 2 * units].astype(BF16)
-        send_ref[1, :, at] = grads[3 * units :].astype(BF16)
-        send_ref[2, :, at] = down[units:].astype(BF16)
-
-
-def weight_grads(own, cots, act):
-    units, dim = act.shape[0] // 2, own.shape[1]
-    grad = jax.ShapeDtypeStruct((units, dim), F32)
+        grads = lax.dot_general(
+            half_ref[: 4 * units], rows_in, LAST, preferred_element_type=F32
+        )
+        down = lax.dot_general(
+            half_ref[4 * units :], rows_grad, LAST, preferred_element_type=F32
+        )
+        for j, (value, begin) in enumerate(((grads, 0), (grads, 2 * units), (down, 0))):
+            keep_ref[j, :, at] = value[begin : begin + units]
+            give_ref[j, :, at] = value[begin + units : begin + 2 * units].astype(BF16)
+        for j, ref in enumerate((gg_ref, gu_ref, gd_ref)):
+            stores.append(
+                pltpu.make_async_copy(keep_ref.at[j, :, at], ref.at[:, at], sems.at[i, j])
+            )
+            stores[-1].start()
+            stores.append(
+                pltpu.make_async_copy(
+                    give_ref.at[j, :, at], send_ref.at[j, :, at], sems.at[i, 3 + j]
+                )
+            )
+            stores[-1].start()
+    for copy in stores:
+        copy.wait()
+
+
+def weight_grads(own, cots):
+    units, dim = cots.shape[0] // 6, own.shape[1]
+    grad = pltpu.HBM((units, dim), F32)
+    hbm = pl.BlockSpec(memory_space=pltpu.HBM)
     return pl.pallas_call(
         grads_kernel,
-        out_shape=(grad, grad, grad, jax.ShapeDtypeStruct((3, units, dim), BF16)),
+        in_specs=[pl.BlockSpec(memory_space=pltpu.VMEM), hbm],
+        out_specs=(hbm, hbm, hbm, hbm),
+        out_shape=(grad, grad, grad, pltpu.HBM((3, units, dim), BF16)),
+        scratch_shapes=[
+            pltpu.VMEM(cots.shape, BF16),
+            pltpu.VMEM((3, units, dim), F32),
+            pltpu.VMEM((3, units, dim), BF16),
+            pltpu.SemaphoreType.DMA((dim // STEP + 1, 6)),
+        ],
         cost_estimate=pl.CostEstimate(
-            flops=2 * 6 * units * dim * act.shape[1], bytes_accessed=7 << 20, transcendentals=0
+            flops=2 * 6 * units * dim * cots.shape[1], bytes_accessed=7 << 20, transcendentals=0
         ),
         compiler_params=pltpu.CompilerParams(vmem_limit_bytes=VMEM_BYTES),
-    )(own, cots, act)
+    )(own, cots)
 
 
 def combine_kernel(back_ref, table_ref, out_ref):
@@ -259,6 +320,20 @@
     )(back, table)
 
 
+ALL = ("far", "pair", "core", "y", "x")
+
+
+def wide_groups():
+    planes = 2 * FAR * PAIR
+    groups = []
+    for first in range(0, planes, 4):
+        for one, two in ((first, first + 2), (first + 3, (first + 5) % planes)):
+            groups.append(
+                [plane * EXPERTS + e for plane in (one, two) for e in range(EXPERTS)]
+            )
+    return groups
+
+
 def exchange(value, axis, groups=None):
     return lax.all_to_all(
         value, axis, split_axis=0, concat_axis=0, tiled=True, axis_index_groups=groups
@@ -266,7 +341,6 @@
 
 
 SWAP = [(0, 1), (1, 0)]
-WIDE = ("pair", "y", "x")
 
 
 def along_z():
@@ -277,17 +351,20 @@
     tok_rows, width = tokens.shape
     dim = w_gate.shape[2]
     mine = (w_gate[0], w_up[0], w_down[0])
-    other = tuple(lax.ppermute(w, "core", SWAP) for w in mine)
-    pair = lax.axis_index("pair").astype(jnp.int32).reshape(1)
-    far = exchange(message(tokens, grad_out, routes, gate_probs), ("far", "pair"), along_z())
-    slots, table = pack(pair, far.reshape(FAR * tok_rows, ROW), width)
-    own = exchange(slots, WIDE).reshape(PAIR, dim, -1)
-    back, cots, act = expert(own, mine, other, width)
-    part = combine(exchange(back, WIDE), table)
+    msg = message(tokens, grad_out, routes, gate_probs)
+    msg, *early = lax.optimization_barrier((msg, *mine))
+    other = [lax.ppermute(w, "core", SWAP) for w in early]
+    pair = (lax.axis_index("pair") + lax.axis_index("core")).astype(jnp.int32).reshape(1) % PAIR
+    far = exchange(msg, ("far", "pair"), along_z())
+    far, *other = lax.optimization_barrier((far, *other))
+    slots, table = pack(pair, far, width)
+    own = exchange(slots, ALL, wide_groups()).reshape(PAIR, dim, -1)
+    back, cots = expert(own, mine, other, width)
+    part = combine(exchange(back, ALL, wide_groups()), table)
     part = exchange(part.reshape(FAR, tok_rows, part.shape[1]), ("far", "pair"), along_z())
     part = lax.optimization_barrier(part.astype(F32))
     grad_in = part.sum(axis=0)[:, :width].astype(BF16)
-    *halves, send = weight_grads(own, cots, act)
+    *halves, send = weight_grads(own, cots)
     send = lax.ppermute(send, "core", SWAP)
     grads = [(half + send[i].astype(F32)).astype(BF16)[None] for i, half in enumerate(halves)]
     return grad_in, *grads

time: 137 us -> 133 us (0.971); the launches traced: 134 us -> 133 us
  blocking collectives: 0 us -> 31.2 us
  waiting for transfers between devices: 26.9 us -> 14.5 us
  local copies, waits for them, and re-layouts: 10.7 us -> 0.02 us
  starting transfers between devices: 81.7 us -> 71.9 us
    all_to_all x0 -> x1, blocking collectives: none -> 31.2 us  [exchange(): lax.all_to_all(value, axis, split_axis=0, concat_axis=0, tiled=True, axis...]
    all_to_all x4 -> x3, waiting for transfers between devices: 26.9 us -> 12.7 us  [exchange(): lax.all_to_all(value, axis, split_axis=0, concat_axis=0, tiled=True, axis...]
    unnamed x30 -> x6, local copies, waits for them, and re-layouts: 10.7 us -> 0.02 us
    all_to_all x4 -> x3, starting transfers between devices: 71.4 us -> 62.5 us  [exchange(): lax.all_to_all(value, axis, split_axis=0, concat_axis=0, tiled=True, axis...]
    ppermute x3, waiting for transfers between devices: 0.01 us -> 1.79 us  [shards(): other = [lax.ppermute(w, 'core', SWAP) for w in early]]
  transfers between devices with their start and end apart: 8 -> 7, of which waited for: 4 -> 4; matrix products, arithmetic and copies ran while one was open for 3% -> 3% of each run, Pallas kernels for 3% -> 3%
where the time goes in v4:
time: 133 us
  starting transfers between devices  71.9 us (54%)
  blocking collectives  31.2 us (23%)
  waiting for transfers between devices  14.5 us (11%)
  Pallas kernels  9.99 us (8%)
  other arithmetic  4.54 us (3%)
    all_to_all x3, starting transfers between devices, exchange(): lax.all_to_all(value, axis, split_axis=0, concat_axis=0, tiled=True, axis...  62.5 us
    all_to_all x1, blocking collectives, exchange(): lax.all_to_all(value, axis, split_axis=0, concat_axis=0, tiled=True, axis...  31.2 us
    all_to_all x3, waiting for transfers between devices, exchange(): lax.all_to_all(value, axis, split_axis=0, concat_axis=0, tiled=True, axis...  12.7 us
    ppermute x3, starting transfers between devices, shards(): other = [lax.ppermute(w, 'core', SWAP) for w in early]  7.46 us
    broadcast_in_dim x1, other arithmetic, shards(): (half + send[i].astype(F32)).astype(BF16)[None]  3.92 us
    pallas_call x1, Pallas kernels, expert(): pl.pallas_call(expert_kernel, out_shape=(pltpu.HBM(back, BF16), jax.Shape...  3.52 us
    pallas_call x1, Pallas kernels, weight_grads(): pl.pallas_call(grads_kernel, in_specs=[pl.BlockSpec(memory_space=pltpu.VM...  3.17 us
  transfers between devices with their start and end apart: 7, of which 4 were waited for; matrix products, arithmetic and copies ran while one was open for 3% of the time, Pallas kernels for 3%

profile of v4, /device:TPU:1, one launch (start us, length us, event | category | flops | bytes accessed | tf_op | source)
XLA Modules:
  0.0 132.9 jit_solution(15565365985769540769)
XLA Ops:
  0.6 1.5 %shard_map.102 = bf16[16,7,4,128]{3,2,1,0:T(4,128)(2,1)} custom-call(bf16[8,192]{1,0:T(8,128)(2,1)} %tokens_ref.1, bf16[8,192]{1,0:T(8,128)(2,1)} %grad_ref.1, s32[4,8]{1,0:T(4,128)} %bitcast.39, f32[4,8]{1,0:T(4,128)} %bitcast.40), custom_call_target="tpu_custom_call" | custom-call | tf_op jit(solution)/shard_map/pallas_call | solution.py:68
  2.1 35.6 %all-to-all-start = ((bf16[16,7,4,128]{3,2,1,0:T(4,128)(2,1)}), bf16[16,7,4,128]{3,2,1,0:T(4,128)(2,1)S(1)}, u32[]{:S(2)}, u32[]{:S(2)}) async-start(bf16[16,7,4,128]{3,2,1,0:T(4,128)(2,1)} %shard_map.102), calls=%async_computation | async-start | bytes 229376 | tf_op jit(solution)/shard_map/all_to_all | solution.py:338
  37.7 3.1 %collective-permute-start = (bf16[96,3072]{1,0:T(8,128)(2,1)}, bf16[96,3072]{1,0:T(8,128)(2,1)S(1)}, u32[]{:S(2)}, u32[]{:S(2)}) collective-permute-start(bf16[96,3072]{1,0:T(8,128)(2,1)} %bitcast.32), channel_id=1, source_target_pairs={{0,16},{16,0},{1,17},{17,1},{2,18},{18,2},{3,19},{19,3},{4,20},{20... | collective-permute-start | bytes 1769480 | tf_op jit(solution)/shard_map/ppermute | solution.py:356
  40.8 1.9 %collective-permute-start.1 = (bf16[96,3072]{1,0:T(8,128)(2,1)}, bf16[96,3072]{1,0:T(8,128)(2,1)S(1)}, u32[]{:S(2)}, u32[]{:S(2)}) collective-permute-start(bf16[96,3072]{1,0:T(8,128)(2,1)} %bitcast.34), channel_id=1, source_target_pairs={{0,16},{16,0},{1,17},{17,1},{2,18},{18,2},{3,19},{19,3},{4,20},{20... | collective-permute-start | bytes 1769480 | tf_op jit(solution)/shard_map/ppermute | solution.py:356
  42.7 2.4 %collective-permute-start.2 = (bf16[96,3072]{1,0:T(8,128)(2,1)}, bf16[96,3072]{1,0:T(8,128)(2,1)S(1)}, u32[]{:S(2)}, u32[]{:S(2)}) collective-permute-start(bf16[96,3072]{1,0:T(8,128)(2,1)} %bitcast.36), channel_id=1, source_target_pairs={{0,16},{16,0},{1,17},{17,1},{2,18},{18,2},{3,19},{19,3},{4,20},{20... | collective-permute-start | bytes 1769480 | tf_op jit(solution)/shard_map/ppermute | solution.py:356
  45.2 0.0 collective-permute-done.hg_ref
  45.2 0.0 collective-permute-done.1.hu_ref
  45.2 1.8 %collective-permute-done.2.hd_ref = bf16[96,3072]{1,0:T(8,128)(2,1)S(1)} collective-permute-done((bf16[96,3072]{1,0:T(8,128)(2,1)}, bf16[96,3072]{1,0:T(8,128)(2,1)S(1)}, u32[]{:S(2)}, u32[]{:S(2)}) %collective-permute-start.2) | collective-permute-done | bytes 589856 | tf_op jit(solution)/shard_map/ppermute | solution.py:356
  47.0 1.9 %all-to-all-done.msg_ref = bf16[16,7,4,128]{3,2,1,0:T(4,128)(2,1)S(1)} async-done(((bf16[16,7,4,128]{3,2,1,0:T(4,128)(2,1)}), bf16[16,7,4,128]{3,2,1,0:T(4,128)(2,1)S(1)}, u32[]{:S(2)}, u32[]{:S(2)}) %all-to-all-start) | async-done | bytes 114720 | tf_op jit(solution)/shard_map/all_to_all | solution.py:338
  48.8 0.7 shard_map.103
  49.6 0.0 copy-start
  49.6 0.0 copy-start.1
  49.6 0.0 copy-start.2
  49.6 31.2 %all_to_all.20 = bf16[32,192,128]{2,1,0:T(8,128)(2,1)S(1)} all-to-all(bf16[32,192,128]{2,1,0:T(8,128)(2,1)S(1)} %get-tuple-element.25), channel_id=1, replica_groups={{0,1,2,3,4,5,6,7,8,9,10,11,12,13,14,15,32,33,34,35,36,37,38,39,40,41,42..., dimensions={0} | all-to-all | bytes 3145728 | tf_op jit(solution)/shard_map/all_to_all | solution.py:338
  80.8 3.5 %shard_map.104 = (bf16[32,96,128]{2,1,0:T(8,128)(2,1)}, bf16[576,128]{1,0:T(8,128)(2,1)S(1)}) custom-call(bf16[2,3072,128]{2,1,0:T(8,128)(2,1)S(1)} %bitcast.30, bf16[96,3072]{1,0:T(8,128)(2,1)S(1)} %bitcast.33, bf16[96,3072]{1,0:T(8,128)(2,1)S(1)} %bitcast.35, bf16[96,3072]{1,0:T(8,128)(2,1)S(1)} %bitcast.37, ...), custom_call_target="tpu_custom_call" | custom-call | flops 754974720 | bytes 6291456 | tf_op jit(solution)/shard_map/pallas_call | solution.py:206
  84.4 5.9 %all-to-all-start.2 = ((bf16[32,96,128]{2,1,0:T(8,128)(2,1)}), bf16[32,96,128]{2,1,0:T(8,128)(2,1)S(1)}, u32[]{:S(2)}, u32[]{:S(2)}) async-start(bf16[32,96,128]{2,1,0:T(8,128)(2,1)} %get-tuple-element.29), calls=%async_computation.2 | async-start | bytes 1572864 | tf_op jit(solution)/shard_map/all_to_all | solution.py:338
  90.3 3.2 %shard_map.106 = (f32[96,3072]{1,0:T(8,128)}, f32[96,3072]{1,0:T(8,128)}, f32[96,3072]{1,0:T(8,128)}, bf16[3,96,3072]{2,1,0:T(8,128)(2,1)}) custom-call(bf16[2,3072,128]{2,1,0:T(8,128)(2,1)S(1)} %bitcast.31, bf16[576,128]{1,0:T(8,128)(2,1)S(1)} %get-tuple-element.31.cots_ref), custom_call_target="tpu_custom_call" | custom-call | flops 452984832 | bytes 7340032 | tf_op jit(solution)/shard_map/pallas_call | solution.py:267
  93.4 1.9 %collective-permute-start.3 = (bf16[3,96,3072]{2,1,0:T(8,128)(2,1)}, bf16[3,96,3072]{2,1,0:T(8,128)(2,1)}, u32[]{:S(2)}, u32[]{:S(2)}) collective-permute-start(bf16[3,96,3072]{2,1,0:T(8,128)(2,1)} %get-tuple-element.33), channel_id=1, source_target_pairs={{0,16},{16,0},{1,17},{17,1},{2,18},{18,2},{3,19},{19,3},{4,20},{20... | collective-permute-start | bytes 5308424 | tf_op jit(solution)/shard_map/ppermute | solution.py:368
  95.4 7.9 %all-to-all-done.2.back_ref = bf16[32,96,128]{2,1,0:T(8,128)(2,1)S(1)} async-done(((bf16[32,96,128]{2,1,0:T(8,128)(2,1)}), bf16[32,96,128]{2,1,0:T(8,128)(2,1)S(1)}, u32[]{:S(2)}, u32[]{:S(2)}) %all-to-all-start.2) | async-done | bytes 786464 | tf_op jit(solution)/shard_map/all_to_all | solution.py:338
  103.2 1.1 shard_map.105
  104.3 21.1 %all-to-all-start.3 = ((bf16[16,8,256]{2,1,0:T(8,128)(2,1)}), bf16[16,8,256]{2,1,0:T(8,128)(2,1)S(1)}, u32[]{:S(2)}, u32[]{:S(2)}) async-start(bf16[16,8,256]{2,1,0:T(8,128)(2,1)} %bitcast.7), calls=%async_computation.3 | async-start | bytes 131072 | tf_op jit(solution)/shard_map/all_to_all | solution.py:338
  125.4 3.9 %fusion.5 = (bf16[1,96,3072]{2,1,0:T(8,128)(2,1)}, bf16[1,96,3072]{2,1,0:T(8,128)(2,1)}, bf16[1,96,3072]{2,1,0:T(8,128)(2,1)}) fusion(f32[96,3072]{1,0:T(8,128)} %get-tuple-element.35, bf16[3,96,3072]{2,1,0:T(8,128)(2,1)} %collective-permute-done.3, f32[96,3072]{1,0:T(8,128)} %get-tuple-element.34, f32[96,3072]{1,0:T(8,128)} %get-tuple-element.32), kind=kLoop, calls=%fused_computation.8 | loop fusion | flops 2654208 | bytes 7077888 | tf_op jit(solution)/shard_map/broadcast_in_dim | solution.py:369
  129.4 2.9 %all-to-all-done.3 = bf16[16,8,256]{2,1,0:T(8,128)(2,1)S(1)} async-done(((bf16[16,8,256]{2,1,0:T(8,128)(2,1)}), bf16[16,8,256]{2,1,0:T(8,128)(2,1)S(1)}, u32[]{:S(2)}, u32[]{:S(2)}) %all-to-all-start.3) | async-done | bytes 65568 | tf_op jit(solution)/shard_map/all_to_all | solution.py:338
  132.3 0.6 reduce_sum.9
  (5 shorter events, 0.0 us)
Async XLA Ops:
  2.1 46.7 %all-to-all-start = ((bf16[16,7,4,128]{3,2,1,0:T(4,128)(2,1)}), bf16[16,7,4,128]{3,2,1,0:T(4,128)(2,1)S(1)}, u32[]{:S(2)}, u32[]{:S(2)}) async-start(bf16[16,7,4,128]{3,2,1,0:T(4,128)(2,1)} %shard_map.102), calls=%async_computation | async-start | bytes 229376 | tf_op jit(solution)/shard_map/all_to_all | solution.py:338
  37.7 7.5 %collective-permute-start = (bf16[96,3072]{1,0:T(8,128)(2,1)}, bf16[96,3072]{1,0:T(8,128)(2,1)S(1)}, u32[]{:S(2)}, u32[]{:S(2)}) collective-permute-start(bf16[96,3072]{1,0:T(8,128)(2,1)} %bitcast.32), channel_id=1, source_target_pairs={{0,16},{16,0},{1,17},{17,1},{2,18},{18,2},{3,19},{19,3},{4,20},{20... | collective-permute-start | bytes 1769480 | tf_op jit(solution)/shard_map/ppermute | solution.py:356
  40.8 4.4 %collective-permute-start.1 = (bf16[96,3072]{1,0:T(8,128)(2,1)}, bf16[96,3072]{1,0:T(8,128)(2,1)S(1)}, u32[]{:S(2)}, u32[]{:S(2)}) collective-permute-start(bf16[96,3072]{1,0:T(8,128)(2,1)} %bitcast.34), channel_id=1, source_target_pairs={{0,16},{16,0},{1,17},{17,1},{2,18},{18,2},{3,19},{19,3},{4,20},{20... | collective-permute-start | bytes 1769480 | tf_op jit(solution)/shard_map/ppermute | solution.py:356
  42.7 4.2 %collective-permute-start.2 = (bf16[96,3072]{1,0:T(8,128)(2,1)}, bf16[96,3072]{1,0:T(8,128)(2,1)S(1)}, u32[]{:S(2)}, u32[]{:S(2)}) collective-permute-start(bf16[96,3072]{1,0:T(8,128)(2,1)} %bitcast.36), channel_id=1, source_target_pairs={{0,16},{16,0},{1,17},{17,1},{2,18},{18,2},{3,19},{19,3},{4,20},{20... | collective-permute-start | bytes 1769480 | tf_op jit(solution)/shard_map/ppermute | solution.py:356
  49.6 31.3 %copy-start = (bf16[1,96,3072]{2,1,0:T(8,128)(2,1)S(1)}, bf16[1,96,3072]{2,1,0:T(8,128)(2,1)}, u32[]{:S(2)}) copy-start(bf16[1,96,3072]{2,1,0:T(8,128)(2,1)} %param.11) | copy-start | bytes 1769476
  49.6 31.3 %copy-start.1 = (bf16[1,96,3072]{2,1,0:T(8,128)(2,1)S(1)}, bf16[1,96,3072]{2,1,0:T(8,128)(2,1)}, u32[]{:S(2)}) copy-start(bf16[1,96,3072]{2,1,0:T(8,128)(2,1)} %param.12) | copy-start | bytes 1769476
  49.6 31.2 %copy-start.2 = (bf16[1,96,3072]{2,1,0:T(8,128)(2,1)S(1)}, bf16[1,96,3072]{2,1,0:T(8,128)(2,1)}, u32[]{:S(2)}) copy-start(bf16[1,96,3072]{2,1,0:T(8,128)(2,1)} %param.13) | copy-start | bytes 1769476
  84.4 18.9 %all-to-all-start.2 = ((bf16[32,96,128]{2,1,0:T(8,128)(2,1)}), bf16[32,96,128]{2,1,0:T(8,128)(2,1)S(1)}, u32[]{:S(2)}, u32[]{:S(2)}) async-start(bf16[32,96,128]{2,1,0:T(8,128)(2,1)} %get-tuple-element.29), calls=%async_computation.2 | async-start | bytes 1572864 | tf_op jit(solution)/shard_map/all_to_all | solution.py:338
  93.4 32.0 %collective-permute-start.3 = (bf16[3,96,3072]{2,1,0:T(8,128)(2,1)}, bf16[3,96,3072]{2,1,0:T(8,128)(2,1)}, u32[]{:S(2)}, u32[]{:S(2)}) collective-permute-start(bf16[3,96,3072]{2,1,0:T(8,128)(2,1)} %get-tuple-element.33), channel_id=1, source_target_pairs={{0,16},{16,0},{1,17},{17,1},{2,18},{18,2},{3,19},{19,3},{4,20},{20... | collective-permute-start | bytes 5308424 | tf_op jit(solution)/shard_map/ppermute | solution.py:368
  104.3 28.0 %all-to-all-start.3 = ((bf16[16,8,256]{2,1,0:T(8,128)(2,1)}), bf16[16,8,256]{2,1,0:T(8,128)(2,1)S(1)}, u32[]{:S(2)}, u32[]{:S(2)}) async-start(bf16[16,8,256]{2,1,0:T(8,128)(2,1)} %bitcast.7), calls=%async_computation.3 | async-start | bytes 131072 | tf_op jit(solution)/shard_map/all_to_all | solution.py:338

commit v5 on v4

--- a/solution.py
+++ b/solution.py
@@ -12,10 +12,12 @@
 PAIR = 2
 BF16 = jnp.bfloat16
 F32 = jnp.float32
-VMEM_BYTES = 24 * 1024 * 1024
+VMEM_BYTES = 12 * 1024 * 1024
 LAST = (((1,), (1,)), ((), ()))
 FIRST = (((0,), (0,)), ((), ()))
-STEP = 768
+STEP = 384
+GATHER_FROM = 10
+SUM_FROM = 8
 
 
 def iota(shape, dim):
@@ -67,7 +69,7 @@
 def message(tokens, grad_out, routes, probs):
     return pl.pallas_call(
         message_kernel,
-        out_shape=jax.ShapeDtypeStruct((FAR, 7, tokens.shape[0] // 2, 128), BF16),
+        out_shape=pltpu.VMEM((FAR, 7, tokens.shape[0] // 2, 128), BF16),
     )(tokens, grad_out, routes.T, probs.T)
 
 
@@ -146,11 +148,16 @@
 
 def expert_kernel(
     own_ref, wg_ref, wu_ref, wd_ref, hg_ref, hu_ref, hd_ref, back_ref, cots_ref,
-    total_ref, sems,
+    down_ref, sems,
 ):
     dim, lanes = own_ref.shape[1:]
     units = wg_ref.shape[0]
     width = back_ref.shape[1] * 2
+    loads = []
+    for i in range(units // 48):
+        part = pl.ds(48 * i, 48)
+        loads.append(pltpu.make_async_copy(hd_ref.at[part], down_ref.at[part], sems.at[i]))
+        loads[-1].start()
 
     def both(at):
         return jnp.concatenate(
@@ -158,13 +165,16 @@
         )
 
     fwd = jnp.zeros((4 * units, lanes), F32)
+    for i in range(dim // STEP):
+        at = pl.ds(i * STEP, STEP)
+        fwd = fwd + jnp.dot(both(at), rows_at(own_ref, at)[0], preferred_element_type=F32)
+    for copy in loads:
+        copy.wait()
     grad_act = jnp.zeros((2 * units, lanes), F32)
     for i in range(dim // STEP):
         at = pl.ds(i * STEP, STEP)
-        rows_in, rows_grad = rows_at(own_ref, at)
-        down = jnp.concatenate([wd_ref[:, at], hd_ref[:, at]], axis=0)
-        fwd = fwd + jnp.dot(both(at), rows_in, preferred_element_type=F32)
-        grad_act = grad_act + jnp.dot(down, rows_grad, preferred_element_type=F32)
+        down = jnp.concatenate([wd_ref[:, at], down_ref[:, at]], axis=0)
+        grad_act = grad_act + jnp.dot(down, rows_at(own_ref, at)[1], preferred_element_type=F32)
     grad_act = turn(grad_act)
     pre_act, up_value = fwd[: 2 * units], fwd[2 * units :]
     sig = jax.nn.sigmoid(pre_act)
@@ -173,12 +183,15 @@
     grad_pre = (grad_act * up_value * slope).astype(BF16)
     grad_upv = (grad_act * silu).astype(BF16)
     cots = jnp.concatenate([grad_pre, grad_upv], axis=0)
-    cots_ref[: 4 * units] = cots
-    cots_ref[4 * units :] = turn(silu * up_value).astype(BF16)
+    activation = turn(silu * up_value).astype(BF16)
+    for half in (0, 1):
+        at = half * units
+        cots_ref[half, :units] = grad_pre[at : at + units]
+        cots_ref[half, units : 2 * units] = grad_upv[at : at + units]
+        cots_ref[half, 2 * units :] = activation[at : at + units]
     wide = jnp.concatenate([cots, turn(cots)], axis=1)
     first = iota((width // 2, lanes), 1) < lanes // 2
     per = STEP // width
-    stores = []
     for i in range(dim // STEP):
         at = pl.ds(i * STEP, STEP)
         total = lax.dot_general(both(at), wide, FIRST, preferred_element_type=F32)
@@ -188,35 +201,26 @@
             lower = total[j * width + width // 2 : (j + 1) * width]
             even = jnp.where(first, upper[:, :lanes], lower[:, lanes:])
             odd = jnp.where(first, upper[:, lanes:], lower[:, :lanes])
-            total_ref[e] = even.astype(BF16)
-            total_ref[EXPERTS + e] = odd.astype(BF16)
-        for p in range(PAIR):
-            part = pl.ds(p * EXPERTS + i * per, per)
-            copy = pltpu.make_async_copy(total_ref.at[part], back_ref.at[part], sems.at[i, p])
-            copy.start()
-            stores.append(copy)
-    for copy in stores:
-        copy.wait()
+            back_ref[e] = even.astype(BF16)
+            back_ref[EXPERTS + e] = odd.astype(BF16)
 
 
 def expert(own, mine, other, width):
     units, dim = mine[0].shape
     lanes = own.shape[2]
     back = (PAIR * EXPERTS, width // 2, lanes)
+    vmem = pl.BlockSpec(memory_space=pltpu.VMEM)
     return pl.pallas_call(
         expert_kernel,
+        in_specs=[vmem] * 6 + [pl.BlockSpec(memory_space=pl.ANY)],
+        scratch_shapes=[
+            pltpu.VMEM((units, dim), BF16),
+            pltpu.SemaphoreType.DMA((units // 48,)),
+        ],
         out_shape=(
-            pltpu.HBM(back, BF16),
-            jax.ShapeDtypeStruct((6 * units, lanes), BF16),
+            pltpu.VMEM(back, BF16),
+            jax.ShapeDtypeStruct((2, 3 * units, lanes), BF16),
         ),
-        out_specs=(
-            pl.BlockSpec(memory_space=pltpu.HBM),
-            pl.BlockSpec(memory_space=pltpu.VMEM),
-        ),
-        scratch_shapes=[
-            pltpu.VMEM(back, BF16),
-            pltpu.SemaphoreType.DMA((dim // STEP, PAIR)),
-        ],
         cost_estimate=pl.CostEstimate(
             flops=2 * 10 * units * dim * lanes, bytes_accessed=6 << 20, transcendentals=0
         ),
@@ -224,62 +228,71 @@
     )(own, *mine, *other)
 
 
-def grads_kernel(
-    own_ref, cots_ref, gg_ref, gu_ref, gd_ref, send_ref, half_ref, keep_ref, give_ref, sems
-):
-    units, dim = gg_ref.shape
-    steps = dim // STEP
-    load = pltpu.make_async_copy(cots_ref, half_ref, sems.at[steps, 0])
-    load.start()
-    load.wait()
+def unit_grads(own_ref, cots_ref, half, at):
+    units = cots_ref.shape[1] // 3
+    rows_in, rows_grad = rows_at(own_ref, at)
+    up = lax.dot_general(
+        cots_ref[half, : 2 * units], rows_in, LAST, preferred_element_type=F32
+    )
+    down = lax.dot_general(
+        cots_ref[half, 2 * units :], rows_grad, LAST, preferred_element_type=F32
+    )
+    return up[:units], up[units:], down
+
+
+def give_kernel(own_ref, cots_ref, send_ref, held_ref, sems):
     stores = []
-    for i in range(steps):
+    for i in range(own_ref.shape[1] // STEP):
         at = pl.ds(i * STEP, STEP)
-        rows_in, rows_grad = rows_at(own_ref, at)
-        grads = lax.dot_general(
-            half_ref[: 4 * units], rows_in, LAST, preferred_element_type=F32
-        )
-        down = lax.dot_general(
-            half_ref[4 * units :], rows_grad, LAST, preferred_element_type=F32
-        )
-        for j, (value, begin) in enumerate(((grads, 0), (grads, 2 * units), (down, 0))):
-            keep_ref[j, :, at] = value[begin : begin + units]
-            give_ref[j, :, at] = value[begin + units : begin + 2 * units].astype(BF16)
-        for j, ref in enumerate((gg_ref, gu_ref, gd_ref)):
-            stores.append(
-                pltpu.make_async_copy(keep_ref.at[j, :, at], ref.at[:, at], sems.at[i, j])
-            )
-            stores[-1].start()
-            stores.append(
-                pltpu.make_async_copy(
-                    give_ref.at[j, :, at], send_ref.at[j, :, at], sems.at[i, 3 + j]
-                )
-            )
-            stores[-1].start()
+        for j, value in enumerate(unit_grads(own_ref, cots_ref, 1, at)):
+            held_ref[j, :, at] = value.astype(BF16)
+        copy = pltpu.make_async_copy(held_ref.at[:, :, at], send_ref.at[:, :, at], sems.at[i])
+        copy.start()
+        stores.append(copy)
     for copy in stores:
         copy.wait()
 
 
+def keep_kernel(own_ref, cots_ref, recv_ref, gg_ref, gu_ref, gd_ref, held_ref, sems):
+    stores = []
+    for i in range(own_ref.shape[1] // STEP):
+        at = pl.ds(i * STEP, STEP)
+        for j, value in enumerate(unit_grads(own_ref, cots_ref, 0, at)):
+            held_ref[j, :, at] = (value + recv_ref[j, :, at].astype(F32)).astype(BF16)
+        for j, ref in enumerate((gg_ref, gu_ref, gd_ref)):
+            copy = pltpu.make_async_copy(held_ref.at[j, :, at], ref.at[:, at], sems.at[i, j])
+            copy.start()
+            stores.append(copy)
+    for copy in stores:
+        copy.wait()
+
+
 def weight_grads(own, cots):
-    units, dim = cots.shape[0] // 6, own.shape[1]
-    grad = pltpu.HBM((units, dim), F32)
+    units, dim = cots.shape[1] // 3, own.shape[1]
+    steps, all_grads = dim // STEP, (3, units, dim)
+    grad = pltpu.HBM((units, dim), BF16)
     hbm = pl.BlockSpec(memory_space=pltpu.HBM)
-    return pl.pallas_call(
-        grads_kernel,
-        in_specs=[pl.BlockSpec(memory_space=pltpu.VMEM), hbm],
-        out_specs=(hbm, hbm, hbm, hbm),
-        out_shape=(grad, grad, grad, pltpu.HBM((3, units, dim), BF16)),
-        scratch_shapes=[
-            pltpu.VMEM(cots.shape, BF16),
-            pltpu.VMEM((3, units, dim), F32),
-            pltpu.VMEM((3, units, dim), BF16),
-            pltpu.SemaphoreType.DMA((dim // STEP + 1, 6)),
-        ],
+    params = dict(
         cost_estimate=pl.CostEstimate(
-            flops=2 * 6 * units * dim * cots.shape[1], bytes_accessed=7 << 20, transcendentals=0
+            flops=2 * 3 * units * dim * cots.shape[2], bytes_accessed=4 << 20, transcendentals=0
         ),
         compiler_params=pltpu.CompilerParams(vmem_limit_bytes=VMEM_BYTES),
+    )
+    send = pl.pallas_call(
+        give_kernel,
+        out_specs=hbm,
+        out_shape=pltpu.HBM(all_grads, BF16),
+        scratch_shapes=[pltpu.VMEM(all_grads, BF16), pltpu.SemaphoreType.DMA((steps,))],
+        **params,
     )(own, cots)
+    recv = lax.ppermute(send, "core", SWAP)
+    return pl.pallas_call(
+        keep_kernel,
+        out_specs=(hbm, hbm, hbm),
+        out_shape=(grad, grad, grad),
+        scratch_shapes=[pltpu.VMEM(all_grads, BF16), pltpu.SemaphoreType.DMA((steps, 3))],
+        **params,
+    )(own, cots, recv)
 
 
 def combine_kernel(back_ref, table_ref, out_ref):
@@ -309,13 +322,16 @@
     total = total[:height] + total[height:]
     total = jnp.concatenate([total[:, :toks], total[:, toks:]], axis=0)
     pad = jnp.zeros((out_ref.shape[1] - 2 * height, toks), F32)
-    out_ref[...] = jnp.transpose(jnp.concatenate([total, pad], axis=0)).astype(BF16)
+    total = jnp.transpose(jnp.concatenate([total, pad], axis=0)).astype(BF16)
+    ahead = (GATHER_FROM - SUM_FROM) % FAR * (toks // FAR)
+    out_ref[ahead:] = total[: toks - ahead]
+    out_ref[:ahead] = total[toks - ahead :]
 
 
 def combine(back, table):
     return pl.pallas_call(
         combine_kernel,
-        out_shape=jax.ShapeDtypeStruct((table.shape[1], 256), BF16),
+        out_shape=pltpu.VMEM((table.shape[1], 256), BF16),
         compiler_params=pltpu.CompilerParams(vmem_limit_bytes=VMEM_BYTES),
     )(back, table)
 
@@ -343,8 +359,8 @@
 SWAP = [(0, 1), (1, 0)]
 
 
-def along_z():
-    return [[(FAR // 2 + i) % FAR * PAIR + p for i in range(FAR)] for p in range(PAIR)]
+def along_z(first):
+    return [[(first + i) % FAR * PAIR + p for i in range(FAR)] for p in range(PAIR)]
 
 
 def shards(tokens, grad_out, routes, gate_probs, w_gate, w_up, w_down):
@@ -355,19 +371,18 @@
     msg, *early = lax.optimization_barrier((msg, *mine))
     other = [lax.ppermute(w, "core", SWAP) for w in early]
     pair = (lax.axis_index("pair") + lax.axis_index("core")).astype(jnp.int32).reshape(1) % PAIR
-    far = exchange(msg, ("far", "pair"), along_z())
+    far = exchange(msg, ("far", "pair"), along_z(GATHER_FROM))
     far, *other = lax.optimization_barrier((far, *other))
     slots, table = pack(pair, far, width)
     own = exchange(slots, ALL, wide_groups()).reshape(PAIR, dim, -1)
     back, cots = expert(own, mine, other, width)
-    part = combine(exchange(back, ALL, wide_groups()), table)
-    part = exchange(part.reshape(FAR, tok_rows, part.shape[1]), ("far", "pair"), along_z())
+    grads = weight_grads(own, cots)
+    back, *grads = lax.optimization_barrier((exchange(back, ALL, wide_groups()), *grads))
+    part = combine(back, table)
+    part = exchange(part.reshape(FAR, tok_rows, part.shape[1]), ("far", "pair"), along_z(SUM_FROM))
     part = lax.optimization_barrier(part.astype(F32))
     grad_in = part.sum(axis=0)[:, :width].astype(BF16)
-    *halves, send = weight_grads(own, cots)
-    send = lax.ppermute(send, "core", SWAP)
-    grads = [(half + send[i].astype(F32)).astype(BF16)[None] for i, half in enumerate(halves)]
-    return grad_in, *grads
+    return grad_in, *(grad[None] for grad in grads)
 
 
 def solution(mesh):

time: 133 us -> 131 us (0.985)
  blocking collectives: 31.2 us -> 58.3 us
  starting transfers between devices: 71.9 us -> 46.1 us
  other arithmetic: 4.54 us -> 0.62 us
  local copies, waits for them, and re-layouts: 0.02 us -> 1.64 us
    all_to_all x1 -> x2, blocking collectives: 31.2 us -> 58.3 us  [exchange(): lax.all_to_all(value, axis, split_axis=0, concat_axis=0, tiled=True, axis...]
    all_to_all x3 -> x2, starting transfers between devices: 62.5 us -> 36.8 us  [exchange(): lax.all_to_all(value, axis, split_axis=0, concat_axis=0, tiled=True, axis...]
    broadcast_in_dim x1 -> x0, other arithmetic: 3.92 us -> none  [shards(): (half + send[i].astype(F32)).astype(BF16)[None]]
    ppermute x1, waiting for transfers between devices: 0.01 us -> 3.87 us  [weight_grads(): recv = lax.ppermute(send, 'core', SWAP)]
    all_to_all x3 -> x2, waiting for transfers between devices: 12.7 us -> 9.32 us  [exchange(): lax.all_to_all(value, axis, split_axis=0, concat_axis=0, tiled=True, axis...]
    unnamed x6 -> x14, local copies, waits for them, and re-layouts: 0.02 us -> 1.64 us
    ppermute x3, waiting for transfers between devices: 1.79 us -> 0.3 us  [shards(): other = [lax.ppermute(w, 'core', SWAP) for w in early]]
    pallas_call x4 -> x5, Pallas kernels: 9.28 us -> 8.92 us  [the longest x1 3.64 us: expert(): pl.pallas_call(expert_kernel, in_specs=[vmem] * 6 + [pl.BlockSpec(memory_...]
  transfers between devices with their start and end apart: 7 -> 6, of which waited for: 4 -> 4; matrix products, arithmetic and copies ran while one was open for 3% -> 0% of each run, Pallas kernels for 3% -> 3%
where the time goes in v5:
time: 131 us
  blocking collectives  58.3 us (45%)
  starting transfers between devices  46.1 us (35%)
  waiting for transfers between devices  13.5 us (10%)
  Pallas kernels  9.63 us (7%)
  local copies, waits for them, and re-layouts  1.64 us (1%)
    all_to_all x2, blocking collectives, exchange(): lax.all_to_all(value, axis, split_axis=0, concat_axis=0, tiled=True, axis...  58.3 us
    all_to_all x2, starting transfers between devices, exchange(): lax.all_to_all(value, axis, split_axis=0, concat_axis=0, tiled=True, axis...  36.8 us
    all_to_all x2, waiting for transfers between devices, exchange(): lax.all_to_all(value, axis, split_axis=0, concat_axis=0, tiled=True, axis...  9.32 us
    ppermute x3, starting transfers between devices, shards(): other = [lax.ppermute(w, 'core', SWAP) for w in early]  7.47 us
    ppermute x1, waiting for transfers between devices, weight_grads(): recv = lax.ppermute(send, 'core', SWAP)  3.87 us
    pallas_call x1, Pallas kernels, expert(): pl.pallas_call(expert_kernel, in_specs=[vmem] * 6 + [pl.BlockSpec(memory_...  3.64 us
  transfers between devices with their start and end apart: 6, of which 4 were waited for; matrix products, arithmetic and copies ran while one was open for 0% of the time, Pallas kernels for 3%

profile of v5, /device:TPU:1, one launch (start us, length us, event | category | flops | bytes accessed | tf_op | source)
XLA Modules:
  0.0 130.6 jit_solution(397174224741456222)
XLA Ops:
  0.6 1.5 %shard_map.102 = bf16[16,7,4,128]{3,2,1,0:T(4,128)(2,1)} custom-call(bf16[8,192]{1,0:T(8,128)(2,1)} %tokens_ref.1, bf16[8,192]{1,0:T(8,128)(2,1)} %grad_ref.1, s32[4,8]{1,0:T(4,128)} %bitcast.23, f32[4,8]{1,0:T(4,128)} %bitcast.24), custom_call_target="tpu_custom_call" | custom-call | tf_op jit(solution)/shard_map/pallas_call | solution.py:70
  2.1 30.9 %all-to-all-start = ((bf16[16,7,4,128]{3,2,1,0:T(4,128)(2,1)}), bf16[16,7,4,128]{3,2,1,0:T(4,128)(2,1)S(1)}, u32[]{:S(2)}, u32[]{:S(2)}) async-start(bf16[16,7,4,128]{3,2,1,0:T(4,128)(2,1)} %shard_map.102), calls=%async_computation | async-start | bytes 229376 | tf_op jit(solution)/shard_map/all_to_all | solution.py:354
  33.0 3.1 %collective-permute-start = (bf16[96,3072]{1,0:T(8,128)(2,1)}, bf16[96,3072]{1,0:T(8,128)(2,1)S(1)}, u32[]{:S(2)}, u32[]{:S(2)}) collective-permute-start(bf16[96,3072]{1,0:T(8,128)(2,1)} %bitcast.15), channel_id=1, source_target_pairs={{0,16},{16,0},{1,17},{17,1},{2,18},{18,2},{3,19},{19,3},{4,20},{20... | collective-permute-start | bytes 1769480 | tf_op jit(solution)/shard_map/ppermute | solution.py:372
  36.2 1.9 %collective-permute-start.1 = (bf16[96,3072]{1,0:T(8,128)(2,1)}, bf16[96,3072]{1,0:T(8,128)(2,1)S(1)}, u32[]{:S(2)}, u32[]{:S(2)}) collective-permute-start(bf16[96,3072]{1,0:T(8,128)(2,1)} %bitcast.17), channel_id=1, source_target_pairs={{0,16},{16,0},{1,17},{17,1},{2,18},{18,2},{3,19},{19,3},{4,20},{20... | collective-permute-start | bytes 1769480 | tf_op jit(solution)/shard_map/ppermute | solution.py:372
  38.1 2.4 %collective-permute-start.2 = (bf16[96,3072]{1,0:T(8,128)(2,1)}, bf16[96,3072]{1,0:T(8,128)(2,1)}, u32[]{:S(2)}, u32[]{:S(2)}) collective-permute-start(bf16[96,3072]{1,0:T(8,128)(2,1)} %bitcast.19), channel_id=1, source_target_pairs={{0,16},{16,0},{1,17},{17,1},{2,18},{18,2},{3,19},{19,3},{4,20},{20... | collective-permute-start | bytes 1769480 | tf_op jit(solution)/shard_map/ppermute | solution.py:372
  40.5 0.0 collective-permute-done.hg_ref
  40.5 0.0 copy-start.3
  40.5 0.8 copy-done.3
  41.3 0.0 collective-permute-done.1.hu_ref
  41.3 0.8 copy-done.5
  42.2 0.3 collective-permute-done.2.hd_ref
  42.4 5.5 %all-to-all-done.msg_ref = bf16[16,7,4,128]{3,2,1,0:T(4,128)(2,1)S(1)} async-done(((bf16[16,7,4,128]{3,2,1,0:T(4,128)(2,1)}), bf16[16,7,4,128]{3,2,1,0:T(4,128)(2,1)S(1)}, u32[]{:S(2)}, u32[]{:S(2)}) %all-to-all-start) | async-done | bytes 114720 | tf_op jit(solution)/shard_map/all_to_all | solution.py:354
  47.9 0.7 shard_map.103
  48.6 31.7 %all_to_all.20 = bf16[32,192,128]{2,1,0:T(8,128)(2,1)S(1)} all-to-all(bf16[32,192,128]{2,1,0:T(8,128)(2,1)S(1)} %get-tuple-element.28), channel_id=1, replica_groups={{0,1,2,3,4,5,6,7,8,9,10,11,12,13,14,15,32,33,34,35,36,37,38,39,40,41,42..., dimensions={0} | all-to-all | bytes 3145728 | tf_op jit(solution)/shard_map/all_to_all | solution.py:354
  80.3 3.6 %shard_map.104 = (bf16[32,96,128]{2,1,0:T(8,128)(2,1)}, bf16[2,288,128]{2,1,0:T(8,128)(2,1)S(1)}) custom-call(bf16[2,3072,128]{2,1,0:T(8,128)(2,1)S(1)} %bitcast.12, bf16[96,3072]{1,0:T(8,128)(2,1)S(1)} %bitcast.16, bf16[96,3072]{1,0:T(8,128)(2,1)S(1)} %bitcast.18, bf16[96,3072]{1,0:T(8,128)(2,1)S(1)} %bitcast.20, bf16[96,3072]{1,0:T(8,128)(2,1)S(1)} %copy-done.4, ...), custom_call_target="tpu_custom_call" | custom-call | flops 754974720 | bytes 6291456 | tf_op jit(solution)/shard_map/pallas_call | solution.py:213
  84.0 5.9 %all-to-all-start.2 = ((bf16[32,96,128]{2,1,0:T(8,128)(2,1)}), bf16[32,96,128]{2,1,0:T(8,128)(2,1)S(1)}, u32[]{:S(2)}, u32[]{:S(2)}) async-start(bf16[32,96,128]{2,1,0:T(8,128)(2,1)} %get-tuple-element.32), calls=%async_computation.2 | async-start | bytes 1572864 | tf_op jit(solution)/shard_map/all_to_all | solution.py:354
  89.9 1.6 %shard_map.105 = bf16[3,96,3072]{2,1,0:T(8,128)(2,1)} custom-call(bf16[2,3072,128]{2,1,0:T(8,128)(2,1)S(1)} %bitcast.13, bf16[2,288,128]{2,1,0:T(8,128)(2,1)S(1)} %get-tuple-element.33.cots_ref), custom_call_target="tpu_custom_call" | custom-call | flops 226492416 | bytes 4194304 | tf_op jit(solution)/shard_map/pallas_call | solution.py:281
  91.5 1.9 %collective-permute-start.3 = (bf16[3,96,3072]{2,1,0:T(8,128)(2,1)}, bf16[3,96,3072]{2,1,0:T(8,128)(2,1)S(1)}, u32[]{:S(2)}, u32[]{:S(2)}) collective-permute-start(bf16[3,96,3072]{2,1,0:T(8,128)(2,1)} %shard_map.105), channel_id=1, source_target_pairs={{0,16},{16,0},{1,17},{17,1},{2,18},{18,2},{3,19},{19,3},{4,20},{20... | collective-permute-start | bytes 5308424 | tf_op jit(solution)/shard_map/ppermute | solution.py:288
  93.4 3.9 %collective-permute-done.3.recv_ref = bf16[3,96,3072]{2,1,0:T(8,128)(2,1)S(1)} collective-permute-done((bf16[3,96,3072]{2,1,0:T(8,128)(2,1)}, bf16[3,96,3072]{2,1,0:T(8,128)(2,1)S(1)}, u32[]{:S(2)}, u32[]{:S(2)}) %collective-permute-start.3) | collective-permute-done | bytes 1769504 | tf_op jit(solution)/shard_map/ppermute | solution.py:288
  97.3 1.7 %shard_map.106 = (bf16[96,3072]{1,0:T(8,128)(2,1)}, bf16[96,3072]{1,0:T(8,128)(2,1)}, bf16[96,3072]{1,0:T(8,128)(2,1)}) custom-call(bf16[2,3072,128]{2,1,0:T(8,128)(2,1)S(1)} %bitcast.14, bf16[2,288,128]{2,1,0:T(8,128)(2,1)S(1)} %get-tuple-element.33.cots_ref, bf16[3,96,3072]{2,1,0:T(8,128)(2,1)S(1)} %collective-permute-done.3.recv_ref), custom_call_target="tpu_custom_call" | custom-call | flops 226492416 | bytes 4194304 | tf_op jit(solution)/shard_map/pallas_call | solution.py:289
  99.0 3.9 %all-to-all-done.2.back_ref = bf16[32,96,128]{2,1,0:T(8,128)(2,1)S(1)} async-done(((bf16[32,96,128]{2,1,0:T(8,128)(2,1)}), bf16[32,96,128]{2,1,0:T(8,128)(2,1)S(1)}, u32[]{:S(2)}, u32[]{:S(2)}) %all-to-all-start.2) | async-done | bytes 786464 | tf_op jit(solution)/shard_map/all_to_all | solution.py:354
  102.9 0.5 shard_map.107
  103.3 26.6 %all_to_all.21 = bf16[16,8,256]{2,1,0:T(8,128)(2,1)S(1)} all-to-all(bf16[16,8,256]{2,1,0:T(8,128)(2,1)S(1)} %bitcast.21), channel_id=1, replica_groups={{512,576,640,704,768,832,896,960,0,64,128,192,256,320,384,448},{544,608..., dimensions={0} | all-to-all | bytes 131072 | tf_op jit(solution)/shard_map/all_to_all | solution.py:354
  129.9 0.6 reduce_sum.9
  (12 shorter events, 0.0 us)
Async XLA Ops:
  2.1 78.2 %copy-start = (bf16[1,96,3072]{2,1,0:T(8,128)(2,1)S(1)}, bf16[1,96,3072]{2,1,0:T(8,128)(2,1)}, u32[]{:S(2)}) copy-start(bf16[1,96,3072]{2,1,0:T(8,128)(2,1)} %param.11) | copy-start | bytes 1769476
  2.1 78.2 %copy-start.1 = (bf16[1,96,3072]{2,1,0:T(8,128)(2,1)S(1)}, bf16[1,96,3072]{2,1,0:T(8,128)(2,1)}, u32[]{:S(2)}) copy-start(bf16[1,96,3072]{2,1,0:T(8,128)(2,1)} %param.12) | copy-start | bytes 1769476
  2.1 78.2 %copy-start.2 = (bf16[1,96,3072]{2,1,0:T(8,128)(2,1)S(1)}, bf16[1,96,3072]{2,1,0:T(8,128)(2,1)}, u32[]{:S(2)}) copy-start(bf16[1,96,3072]{2,1,0:T(8,128)(2,1)} %param.13) | copy-start | bytes 1769476
  2.1 45.8 %all-to-all-start = ((bf16[16,7,4,128]{3,2,1,0:T(4,128)(2,1)}), bf16[16,7,4,128]{3,2,1,0:T(4,128)(2,1)S(1)}, u32[]{:S(2)}, u32[]{:S(2)}) async-start(bf16[16,7,4,128]{3,2,1,0:T(4,128)(2,1)} %shard_map.102), calls=%async_computation | async-start | bytes 229376 | tf_op jit(solution)/shard_map/all_to_all | solution.py:354
  33.0 7.5 %collective-permute-start = (bf16[96,3072]{1,0:T(8,128)(2,1)}, bf16[96,3072]{1,0:T(8,128)(2,1)S(1)}, u32[]{:S(2)}, u32[]{:S(2)}) collective-permute-start(bf16[96,3072]{1,0:T(8,128)(2,1)} %bitcast.15), channel_id=1, source_target_pairs={{0,16},{16,0},{1,17},{17,1},{2,18},{18,2},{3,19},{19,3},{4,20},{20... | collective-permute-start | bytes 1769480 | tf_op jit(solution)/shard_map/ppermute | solution.py:372
  36.2 5.2 %collective-permute-start.1 = (bf16[96,3072]{1,0:T(8,128)(2,1)}, bf16[96,3072]{1,0:T(8,128)(2,1)S(1)}, u32[]{:S(2)}, u32[]{:S(2)}) collective-permute-start(bf16[96,3072]{1,0:T(8,128)(2,1)} %bitcast.17), channel_id=1, source_target_pairs={{0,16},{16,0},{1,17},{17,1},{2,18},{18,2},{3,19},{19,3},{4,20},{20... | collective-permute-start | bytes 1769480 | tf_op jit(solution)/shard_map/ppermute | solution.py:372
  38.1 4.4 %collective-permute-start.2 = (bf16[96,3072]{1,0:T(8,128)(2,1)}, bf16[96,3072]{1,0:T(8,128)(2,1)}, u32[]{:S(2)}, u32[]{:S(2)}) collective-permute-start(bf16[96,3072]{1,0:T(8,128)(2,1)} %bitcast.19), channel_id=1, source_target_pairs={{0,16},{16,0},{1,17},{17,1},{2,18},{18,2},{3,19},{19,3},{4,20},{20... | collective-permute-start | bytes 1769480 | tf_op jit(solution)/shard_map/ppermute | solution.py:372
  40.5 0.8 copy-start.3
  41.3 0.8 copy-start.5
  47.9 32.4 %copy-start.4 = (bf16[96,3072]{1,0:T(8,128)(2,1)S(1)}, bf16[96,3072]{1,0:T(8,128)(2,1)}, u32[]{:S(2)}) copy-start(bf16[96,3072]{1,0:T(8,128)(2,1)} %copy-done.3) | copy-start | bytes 1769476
  47.9 32.4 %copy-start.6 = (bf16[96,3072]{1,0:T(8,128)(2,1)S(1)}, bf16[96,3072]{1,0:T(8,128)(2,1)}, u32[]{:S(2)}) copy-start(bf16[96,3072]{1,0:T(8,128)(2,1)} %copy-done.5) | copy-start | bytes 1769476
  84.0 18.9 %all-to-all-start.2 = ((bf16[32,96,128]{2,1,0:T(8,128)(2,1)}), bf16[32,96,128]{2,1,0:T(8,128)(2,1)S(1)}, u32[]{:S(2)}, u32[]{:S(2)}) async-start(bf16[32,96,128]{2,1,0:T(8,128)(2,1)} %get-tuple-element.32), calls=%async_computation.2 | async-start | bytes 1572864 | tf_op jit(solution)/shard_map/all_to_all | solution.py:354
  91.5 5.8 %collective-permute-start.3 = (bf16[3,96,3072]{2,1,0:T(8,128)(2,1)}, bf16[3,96,3072]{2,1,0:T(8,128)(2,1)S(1)}, u32[]{:S(2)}, u32[]{:S(2)}) collective-permute-start(bf16[3,96,3072]{2,1,0:T(8,128)(2,1)} %shard_map.105), channel_id=1, source_target_pairs={{0,16},{16,0},{1,17},{17,1},{2,18},{18,2},{3,19},{19,3},{4,20},{20... | collective-permute-start | bytes 5308424 | tf_op jit(solution)/shard_map/ppermute | solution.py:288

commit v6 on v5

--- a/solution.py
+++ b/solution.py
@@ -154,8 +154,8 @@
     units = wg_ref.shape[0]
     width = back_ref.shape[1] * 2
     loads = []
-    for i in range(units // 48):
-        part = pl.ds(48 * i, 48)
+    for i in range(units // 96):
+        part = pl.ds(96 * i, 96)
         loads.append(pltpu.make_async_copy(hd_ref.at[part], down_ref.at[part], sems.at[i]))
         loads[-1].start()
 
@@ -215,7 +215,7 @@
         in_specs=[vmem] * 6 + [pl.BlockSpec(memory_space=pl.ANY)],
         scratch_shapes=[
             pltpu.VMEM((units, dim), BF16),
-            pltpu.SemaphoreType.DMA((units // 48,)),
+            pltpu.SemaphoreType.DMA((units // 96,)),
         ],
         out_shape=(
             pltpu.VMEM(back, BF16),
@@ -343,7 +343,7 @@
     planes = 2 * FAR * PAIR
     groups = []
     for first in range(0, planes, 4):
-        for one, two in ((first, first + 2), (first + 3, (first + 5) % planes)):
+        for one, two in ((first, first + 2), (first + 1, first + 3)):
             groups.append(
                 [plane * EXPERTS + e for plane in (one, two) for e in range(EXPERTS)]
             )
@@ -370,7 +370,7 @@
     msg = message(tokens, grad_out, routes, gate_probs)
     msg, *early = lax.optimization_barrier((msg, *mine))
     other = [lax.ppermute(w, "core", SWAP) for w in early]
-    pair = (lax.axis_index("pair") + lax.axis_index("core")).astype(jnp.int32).reshape(1) % PAIR
+    pair = lax.axis_index("pair").astype(jnp.int32).reshape(1)
     far = exchange(msg, ("far", "pair"), along_z(GATHER_FROM))
     far, *other = lax.optimization_barrier((far, *other))
     slots, table = pack(pair, far, width)

time: 131 us -> 126 us (0.962)
  the two profiles are of different devices: /device:TPU:1 before, /device:TPU:2 now
where the time goes in v6:
time: 126 us
  blocking collectives  55.6 us (44%)
  starting transfers between devices  44 us (35%)
  waiting for transfers between devices  13.2 us (10%)
  Pallas kernels  9.69 us (8%)
  local copies, waits for them, and re-layouts  1.64 us (1%)
    all_to_all x2, blocking collectives, exchange(): lax.all_to_all(value, axis, split_axis=0, concat_axis=0, tiled=True, axis...  55.6 us
    all_to_all x2, starting transfers between devices, exchange(): lax.all_to_all(value, axis, split_axis=0, concat_axis=0, tiled=True, axis...  35.9 us
    all_to_all x2, waiting for transfers between devices, exchange(): lax.all_to_all(value, axis, split_axis=0, concat_axis=0, tiled=True, axis...  8.71 us
    ppermute x3, starting transfers between devices, shards(): other = [lax.ppermute(w, 'core', SWAP) for w in early]  6.24 us
    ppermute x1, waiting for transfers between devices, weight_grads(): recv = lax.ppermute(send, 'core', SWAP)  3.87 us
    pallas_call x1, Pallas kernels, expert(): pl.pallas_call(expert_kernel, in_specs=[vmem] * 6 + [pl.BlockSpec(memory_...  3.7 us
  transfers between devices with their start and end apart: 6, of which 4 were waited for; matrix products, arithmetic and copies ran while one was open for 0% of the time, Pallas kernels for 3%

profile of v6, /device:TPU:2, one launch (start us, length us, event | category | flops | bytes accessed | tf_op | source)
XLA Modules:
  0.0 125.6 jit_solution(17976384524644449451)
XLA Ops:
  0.6 1.5 %shard_map.102 = bf16[16,7,4,128]{3,2,1,0:T(4,128)(2,1)} custom-call(bf16[8,192]{1,0:T(8,128)(2,1)} %tokens_ref.1, bf16[8,192]{1,0:T(8,128)(2,1)} %grad_ref.1, s32[4,8]{1,0:T(4,128)} %bitcast.23, f32[4,8]{1,0:T(4,128)} %bitcast.24), custom_call_target="tpu_custom_call" | custom-call | tf_op jit(solution)/shard_map/pallas_call | solution.py:70
  2.1 30.6 %all-to-all-start = ((bf16[16,7,4,128]{3,2,1,0:T(4,128)(2,1)}), bf16[16,7,4,128]{3,2,1,0:T(4,128)(2,1)S(1)}, u32[]{:S(2)}, u32[]{:S(2)}) async-start(bf16[16,7,4,128]{3,2,1,0:T(4,128)(2,1)} %shard_map.102), calls=%async_computation | async-start | bytes 229376 | tf_op jit(solution)/shard_map/all_to_all | solution.py:354
  32.7 1.9 %collective-permute-start = (bf16[96,3072]{1,0:T(8,128)(2,1)}, bf16[96,3072]{1,0:T(8,128)(2,1)S(1)}, u32[]{:S(2)}, u32[]{:S(2)}) collective-permute-start(bf16[96,3072]{1,0:T(8,128)(2,1)} %bitcast.15), channel_id=1, source_target_pairs={{0,16},{16,0},{1,17},{17,1},{2,18},{18,2},{3,19},{19,3},{4,20},{20... | collective-permute-start | bytes 1769480 | tf_op jit(solution)/shard_map/ppermute | solution.py:372
  34.7 2.4 %collective-permute-start.1 = (bf16[96,3072]{1,0:T(8,128)(2,1)}, bf16[96,3072]{1,0:T(8,128)(2,1)S(1)}, u32[]{:S(2)}, u32[]{:S(2)}) collective-permute-start(bf16[96,3072]{1,0:T(8,128)(2,1)} %bitcast.17), channel_id=1, source_target_pairs={{0,16},{16,0},{1,17},{17,1},{2,18},{18,2},{3,19},{19,3},{4,20},{20... | collective-permute-start | bytes 1769480 | tf_op jit(solution)/shard_map/ppermute | solution.py:372
  37.1 1.9 %collective-permute-start.2 = (bf16[96,3072]{1,0:T(8,128)(2,1)}, bf16[96,3072]{1,0:T(8,128)(2,1)}, u32[]{:S(2)}, u32[]{:S(2)}) collective-permute-start(bf16[96,3072]{1,0:T(8,128)(2,1)} %bitcast.19), channel_id=1, source_target_pairs={{0,16},{16,0},{1,17},{17,1},{2,18},{18,2},{3,19},{19,3},{4,20},{20... | collective-permute-start | bytes 1769480 | tf_op jit(solution)/shard_map/ppermute | solution.py:372
  39.0 0.0 collective-permute-done.hg_ref
  39.0 0.0 copy-start.3
  39.0 0.8 copy-done.3
  39.8 0.0 collective-permute-done.1.hu_ref
  39.8 0.8 copy-done.5
  40.7 0.7 collective-permute-done.2.hd_ref
  41.3 6.9 %all-to-all-done.msg_ref = bf16[16,7,4,128]{3,2,1,0:T(4,128)(2,1)S(1)} async-done(((bf16[16,7,4,128]{3,2,1,0:T(4,128)(2,1)}), bf16[16,7,4,128]{3,2,1,0:T(4,128)(2,1)S(1)}, u32[]{:S(2)}, u32[]{:S(2)}) %all-to-all-start) | async-done | bytes 114720 | tf_op jit(solution)/shard_map/all_to_all | solution.py:354
  48.2 0.7 shard_map.103
  48.9 27.9 %all_to_all.20 = bf16[32,192,128]{2,1,0:T(8,128)(2,1)S(1)} all-to-all(bf16[32,192,128]{2,1,0:T(8,128)(2,1)S(1)} %get-tuple-element.28), channel_id=1, replica_groups={{0,1,2,3,4,5,6,7,8,9,10,11,12,13,14,15,32,33,34,35,36,37,38,39,40,41,42..., dimensions={0} | all-to-all | bytes 3145728 | tf_op jit(solution)/shard_map/all_to_all | solution.py:354
  76.8 3.7 %shard_map.104 = (bf16[32,96,128]{2,1,0:T(8,128)(2,1)}, bf16[2,288,128]{2,1,0:T(8,128)(2,1)S(1)}) custom-call(bf16[2,3072,128]{2,1,0:T(8,128)(2,1)S(1)} %bitcast.12, bf16[96,3072]{1,0:T(8,128)(2,1)S(1)} %bitcast.16, bf16[96,3072]{1,0:T(8,128)(2,1)S(1)} %bitcast.18, bf16[96,3072]{1,0:T(8,128)(2,1)S(1)} %bitcast.20, bf16[96,3072]{1,0:T(8,128)(2,1)S(1)} %copy-done.4, ...), custom_call_target="tpu_custom_call" | custom-call | flops 754974720 | bytes 6291456 | tf_op jit(solution)/shard_map/pallas_call | solution.py:213
  80.5 5.2 %all-to-all-start.2 = ((bf16[32,96,128]{2,1,0:T(8,128)(2,1)}), bf16[32,96,128]{2,1,0:T(8,128)(2,1)S(1)}, u32[]{:S(2)}, u32[]{:S(2)}) async-start(bf16[32,96,128]{2,1,0:T(8,128)(2,1)} %get-tuple-element.32), calls=%async_computation.2 | async-start | bytes 1572864 | tf_op jit(solution)/shard_map/all_to_all | solution.py:354
  85.8 1.6 %shard_map.105 = bf16[3,96,3072]{2,1,0:T(8,128)(2,1)} custom-call(bf16[2,3072,128]{2,1,0:T(8,128)(2,1)S(1)} %bitcast.13, bf16[2,288,128]{2,1,0:T(8,128)(2,1)S(1)} %get-tuple-element.33.cots_ref), custom_call_target="tpu_custom_call" | custom-call | flops 226492416 | bytes 4194304 | tf_op jit(solution)/shard_map/pallas_call | solution.py:281
  87.4 1.9 %collective-permute-start.3 = (bf16[3,96,3072]{2,1,0:T(8,128)(2,1)}, bf16[3,96,3072]{2,1,0:T(8,128)(2,1)S(1)}, u32[]{:S(2)}, u32[]{:S(2)}) collective-permute-start(bf16[3,96,3072]{2,1,0:T(8,128)(2,1)} %shard_map.105), channel_id=1, source_target_pairs={{0,16},{16,0},{1,17},{17,1},{2,18},{18,2},{3,19},{19,3},{4,20},{20... | collective-permute-start | bytes 5308424 | tf_op jit(solution)/shard_map/ppermute | solution.py:288
  89.4 3.9 %collective-permute-done.3.recv_ref = bf16[3,96,3072]{2,1,0:T(8,128)(2,1)S(1)} collective-permute-done((bf16[3,96,3072]{2,1,0:T(8,128)(2,1)}, bf16[3,96,3072]{2,1,0:T(8,128)(2,1)S(1)}, u32[]{:S(2)}, u32[]{:S(2)}) %collective-permute-start.3) | collective-permute-done | bytes 1769504 | tf_op jit(solution)/shard_map/ppermute | solution.py:288
  93.2 1.7 %shard_map.106 = (bf16[96,3072]{1,0:T(8,128)(2,1)}, bf16[96,3072]{1,0:T(8,128)(2,1)}, bf16[96,3072]{1,0:T(8,128)(2,1)}) custom-call(bf16[2,3072,128]{2,1,0:T(8,128)(2,1)S(1)} %bitcast.14, bf16[2,288,128]{2,1,0:T(8,128)(2,1)S(1)} %get-tuple-element.33.cots_ref, bf16[3,96,3072]{2,1,0:T(8,128)(2,1)S(1)} %collective-permute-done.3.recv_ref), custom_call_target="tpu_custom_call" | custom-call | flops 226492416 | bytes 4194304 | tf_op jit(solution)/shard_map/pallas_call | solution.py:289
  95.0 1.8 %all-to-all-done.2.back_ref = bf16[32,96,128]{2,1,0:T(8,128)(2,1)S(1)} async-done(((bf16[32,96,128]{2,1,0:T(8,128)(2,1)}), bf16[32,96,128]{2,1,0:T(8,128)(2,1)S(1)}, u32[]{:S(2)}, u32[]{:S(2)}) %all-to-all-start.2) | async-done | bytes 786464 | tf_op jit(solution)/shard_map/all_to_all | solution.py:354
  96.8 0.5 shard_map.107
  97.3 27.7 %all_to_all.21 = bf16[16,8,256]{2,1,0:T(8,128)(2,1)S(1)} all-to-all(bf16[16,8,256]{2,1,0:T(8,128)(2,1)S(1)} %bitcast.21), channel_id=1, replica_groups={{512,576,640,704,768,832,896,960,0,64,128,192,256,320,384,448},{544,608..., dimensions={0} | all-to-all | bytes 131072 | tf_op jit(solution)/shard_map/all_to_all | solution.py:354
  125.0 0.6 reduce_sum.9
  (12 shorter events, 0.0 us)
Async XLA Ops:
  2.1 74.7 %copy-start = (bf16[1,96,3072]{2,1,0:T(8,128)(2,1)S(1)}, bf16[1,96,3072]{2,1,0:T(8,128)(2,1)}, u32[]{:S(2)}) copy-start(bf16[1,96,3072]{2,1,0:T(8,128)(2,1)} %param.11) | copy-start | bytes 1769476
  2.1 74.7 %copy-start.1 = (bf16[1,96,3072]{2,1,0:T(8,128)(2,1)S(1)}, bf16[1,96,3072]{2,1,0:T(8,128)(2,1)}, u32[]{:S(2)}) copy-start(bf16[1,96,3072]{2,1,0:T(8,128)(2,1)} %param.12) | copy-start | bytes 1769476
  2.1 74.7 %copy-start.2 = (bf16[1,96,3072]{2,1,0:T(8,128)(2,1)S(1)}, bf16[1,96,3072]{2,1,0:T(8,128)(2,1)}, u32[]{:S(2)}) copy-start(bf16[1,96,3072]{2,1,0:T(8,128)(2,1)} %param.13) | copy-start | bytes 1769476
  2.1 46.1 %all-to-all-start = ((bf16[16,7,4,128]{3,2,1,0:T(4,128)(2,1)}), bf16[16,7,4,128]{3,2,1,0:T(4,128)(2,1)S(1)}, u32[]{:S(2)}, u32[]{:S(2)}) async-start(bf16[16,7,4,128]{3,2,1,0:T(4,128)(2,1)} %shard_map.102), calls=%async_computation | async-start | bytes 229376 | tf_op jit(solution)/shard_map/all_to_all | solution.py:354
  32.7 6.3 %collective-permute-start = (bf16[96,3072]{1,0:T(8,128)(2,1)}, bf16[96,3072]{1,0:T(8,128)(2,1)S(1)}, u32[]{:S(2)}, u32[]{:S(2)}) collective-permute-start(bf16[96,3072]{1,0:T(8,128)(2,1)} %bitcast.15), channel_id=1, source_target_pairs={{0,16},{16,0},{1,17},{17,1},{2,18},{18,2},{3,19},{19,3},{4,20},{20... | collective-permute-start | bytes 1769480 | tf_op jit(solution)/shard_map/ppermute | solution.py:372
  34.7 5.2 %collective-permute-start.1 = (bf16[96,3072]{1,0:T(8,128)(2,1)}, bf16[96,3072]{1,0:T(8,128)(2,1)S(1)}, u32[]{:S(2)}, u32[]{:S(2)}) collective-permute-start(bf16[96,3072]{1,0:T(8,128)(2,1)} %bitcast.17), channel_id=1, source_target_pairs={{0,16},{16,0},{1,17},{17,1},{2,18},{18,2},{3,19},{19,3},{4,20},{20... | collective-permute-start | bytes 1769480 | tf_op jit(solution)/shard_map/ppermute | solution.py:372
  37.1 4.2 %collective-permute-start.2 = (bf16[96,3072]{1,0:T(8,128)(2,1)}, bf16[96,3072]{1,0:T(8,128)(2,1)}, u32[]{:S(2)}, u32[]{:S(2)}) collective-permute-start(bf16[96,3072]{1,0:T(8,128)(2,1)} %bitcast.19), channel_id=1, source_target_pairs={{0,16},{16,0},{1,17},{17,1},{2,18},{18,2},{3,19},{19,3},{4,20},{20... | collective-permute-start | bytes 1769480 | tf_op jit(solution)/shard_map/ppermute | solution.py:372
  39.0 0.8 copy-start.3
  39.8 0.8 copy-start.5
  48.2 28.6 %copy-start.4 = (bf16[96,3072]{1,0:T(8,128)(2,1)S(1)}, bf16[96,3072]{1,0:T(8,128)(2,1)}, u32[]{:S(2)}) copy-start(bf16[96,3072]{1,0:T(8,128)(2,1)} %copy-done.3) | copy-start | bytes 1769476
  48.2 28.6 %copy-start.6 = (bf16[96,3072]{1,0:T(8,128)(2,1)S(1)}, bf16[96,3072]{1,0:T(8,128)(2,1)}, u32[]{:S(2)}) copy-start(bf16[96,3072]{1,0:T(8,128)(2,1)} %copy-done.5) | copy-start | bytes 1769476
  80.5 16.2 %all-to-all-start.2 = ((bf16[32,96,128]{2,1,0:T(8,128)(2,1)}), bf16[32,96,128]{2,1,0:T(8,128)(2,1)S(1)}, u32[]{:S(2)}, u32[]{:S(2)}) async-start(bf16[32,96,128]{2,1,0:T(8,128)(2,1)} %get-tuple-element.32), calls=%async_computation.2 | async-start | bytes 1572864 | tf_op jit(solution)/shard_map/all_to_all | solution.py:354
  87.4 5.8 %collective-permute-start.3 = (bf16[3,96,3072]{2,1,0:T(8,128)(2,1)}, bf16[3,96,3072]{2,1,0:T(8,128)(2,1)S(1)}, u32[]{:S(2)}, u32[]{:S(2)}) collective-permute-start(bf16[3,96,3072]{2,1,0:T(8,128)(2,1)} %shard_map.105), channel_id=1, source_target_pairs={{0,16},{16,0},{1,17},{17,1},{2,18},{18,2},{3,19},{19,3},{4,20},{20... | collective-permute-start | bytes 5308424 | tf_op jit(solution)/shard_map/ppermute | solution.py:288

commit v7 on v6

--- a/solution.py
+++ b/solution.py
@@ -321,19 +321,37 @@
         )
     total = total[:height] + total[height:]
     total = jnp.concatenate([total[:, :toks], total[:, toks:]], axis=0)
-    pad = jnp.zeros((out_ref.shape[1] - 2 * height, toks), F32)
-    total = jnp.transpose(jnp.concatenate([total, pad], axis=0)).astype(BF16)
+    pad = jnp.zeros((256 - 2 * height, toks), F32)
+    total = jnp.transpose(jnp.concatenate([total, pad], axis=0))
     ahead = (GATHER_FROM - SUM_FROM) % FAR * (toks // FAR)
-    out_ref[ahead:] = total[: toks - ahead]
-    out_ref[:ahead] = total[toks - ahead :]
+    total = jnp.concatenate([total[toks - ahead :], total[: toks - ahead]], axis=0)
+    shape = (FAR, 2, toks // FAR // 2, 128)
+    low = total[:, 128:].reshape(shape)
+    out_ref[:, 0:2] = total[:, :128].reshape(shape).astype(BF16)
+    out_ref[:, 2] = (low[:, 0] + pltpu.roll(low[:, 1], 64, 2)).astype(BF16)
 
 
 def combine(back, table):
     return pl.pallas_call(
         combine_kernel,
-        out_shape=pltpu.VMEM((table.shape[1], 256), BF16),
+        out_shape=pltpu.VMEM((FAR, 3, table.shape[1] // FAR // 2, 128), BF16),
         compiler_params=pltpu.CompilerParams(vmem_limit_bytes=VMEM_BYTES),
     )(back, table)
+
+
+def sum_kernel(parts_ref, out_ref):
+    total = parts_ref[0].astype(F32)
+    for i in range(1, parts_ref.shape[0]):
+        total = total + parts_ref[i].astype(F32)
+    low = jnp.concatenate([total[2], pltpu.roll(total[2], 64, 1)], axis=0)
+    out_ref[:, :128] = jnp.concatenate([total[0], total[1]], axis=0).astype(BF16)
+    out_ref[:, 128:] = low[:, : out_ref.shape[1] - 128].astype(BF16)
+
+
+def add_parts(parts, tok_rows, width):
+    return pl.pallas_call(
+        sum_kernel, out_shape=jax.ShapeDtypeStruct((tok_rows, width), BF16)
+    )(parts)
 
 
 ALL = ("far", "pair", "core", "y", "x")
@@ -379,9 +397,8 @@
     grads = weight_grads(own, cots)
     back, *grads = lax.optimization_barrier((exchange(back, ALL, wide_groups()), *grads))
     part = combine(back, table)
-    part = exchange(part.reshape(FAR, tok_rows, part.shape[1]), ("far", "pair"), along_z(SUM_FROM))
-    part = lax.optimization_barrier(part.astype(F32))
-    grad_in = part.sum(axis=0)[:, :width].astype(BF16)
+    part = exchange(part, ("far", "pair"), along_z(SUM_FROM))
+    grad_in = add_parts(part, tok_rows, width)
     return grad_in, *(grad[None] for grad in grads)
 
 

time: 126 us -> 127 us (level)
  Pallas kernels: 9.69 us -> 11.3 us
    pallas_call x1 -> x2, Pallas kernels: 0.47 us -> 2.02 us  [the longest x1 1.48 us: add_parts(): pl.pallas_call(sum_kernel, out_shape=jax.ShapeDtypeStruct((tok_rows, widt...]
where the time goes in v7:
time: 127 us; the launch traced here: 126 us
  blocking collectives  55 us (43%)
  starting transfers between devices  44 us (35%)
  waiting for transfers between devices  13.2 us (10%)
  Pallas kernels  11.3 us (9%)
  local copies, waits for them, and re-layouts  1.64 us (1%)
    all_to_all x2, blocking collectives, exchange(): lax.all_to_all(value, axis, split_axis=0, concat_axis=0, tiled=True, axis...  55 us
    all_to_all x2, starting transfers between devices, exchange(): lax.all_to_all(value, axis, split_axis=0, concat_axis=0, tiled=True, axis...  35.9 us
    all_to_all x2, waiting for transfers between devices, exchange(): lax.all_to_all(value, axis, split_axis=0, concat_axis=0, tiled=True, axis...  8.65 us
    ppermute x3, starting transfers between devices, shards(): other = [lax.ppermute(w, 'core', SWAP) for w in early]  6.24 us
    ppermute x1, waiting for transfers between devices, weight_grads(): recv = lax.ppermute(send, 'core', SWAP)  3.87 us
    pallas_call x1, Pallas kernels, expert(): pl.pallas_call(expert_kernel, in_specs=[vmem] * 6 + [pl.BlockSpec(memory_...  3.7 us
  transfers between devices with their start and end apart: 6, of which 4 were waited for; matrix products, arithmetic and copies ran while one was open for 0% of the time, Pallas kernels for 3%

profile of v7, /device:TPU:2, one launch (start us, length us, event | category | flops | bytes accessed | tf_op | source)
XLA Modules:
  0.0 125.9 jit_solution(6839404839125783902)
XLA Ops:
  0.6 1.5 %shard_map.102 = bf16[16,7,4,128]{3,2,1,0:T(4,128)(2,1)} custom-call(bf16[8,192]{1,0:T(8,128)(2,1)} %tokens_ref.1, bf16[8,192]{1,0:T(8,128)(2,1)} %grad_ref.1, s32[4,8]{1,0:T(4,128)} %bitcast.19, f32[4,8]{1,0:T(4,128)} %bitcast.20), custom_call_target="tpu_custom_call" | custom-call | tf_op jit(solution)/shard_map/pallas_call | solution.py:70
  2.1 30.6 %all-to-all-start = ((bf16[16,7,4,128]{3,2,1,0:T(4,128)(2,1)}), bf16[16,7,4,128]{3,2,1,0:T(4,128)(2,1)S(1)}, u32[]{:S(2)}, u32[]{:S(2)}) async-start(bf16[16,7,4,128]{3,2,1,0:T(4,128)(2,1)} %shard_map.102), calls=%async_computation | async-start | bytes 229376 | tf_op jit(solution)/shard_map/all_to_all | solution.py:372
  32.7 1.9 %collective-permute-start = (bf16[96,3072]{1,0:T(8,128)(2,1)}, bf16[96,3072]{1,0:T(8,128)(2,1)S(1)}, u32[]{:S(2)}, u32[]{:S(2)}) collective-permute-start(bf16[96,3072]{1,0:T(8,128)(2,1)} %bitcast.13), channel_id=1, source_target_pairs={{0,16},{16,0},{1,17},{17,1},{2,18},{18,2},{3,19},{19,3},{4,20},{20... | collective-permute-start | bytes 1769480 | tf_op jit(solution)/shard_map/ppermute | solution.py:390
  34.7 2.4 %collective-permute-start.1 = (bf16[96,3072]{1,0:T(8,128)(2,1)}, bf16[96,3072]{1,0:T(8,128)(2,1)S(1)}, u32[]{:S(2)}, u32[]{:S(2)}) collective-permute-start(bf16[96,3072]{1,0:T(8,128)(2,1)} %bitcast.15), channel_id=1, source_target_pairs={{0,16},{16,0},{1,17},{17,1},{2,18},{18,2},{3,19},{19,3},{4,20},{20... | collective-permute-start | bytes 1769480 | tf_op jit(solution)/shard_map/ppermute | solution.py:390
  37.1 1.9 %collective-permute-start.2 = (bf16[96,3072]{1,0:T(8,128)(2,1)}, bf16[96,3072]{1,0:T(8,128)(2,1)}, u32[]{:S(2)}, u32[]{:S(2)}) collective-permute-start(bf16[96,3072]{1,0:T(8,128)(2,1)} %bitcast.17), channel_id=1, source_target_pairs={{0,16},{16,0},{1,17},{17,1},{2,18},{18,2},{3,19},{19,3},{4,20},{20... | collective-permute-start | bytes 1769480 | tf_op jit(solution)/shard_map/ppermute | solution.py:390
  39.0 0.0 collective-permute-done.hg_ref
  39.0 0.0 copy-start.3
  39.0 0.8 copy-done.3
  39.8 0.0 collective-permute-done.1.hu_ref
  39.8 0.8 copy-done.5
  40.7 0.7 collective-permute-done.2.hd_ref
  41.3 6.9 %all-to-all-done.msg_ref = bf16[16,7,4,128]{3,2,1,0:T(4,128)(2,1)S(1)} async-done(((bf16[16,7,4,128]{3,2,1,0:T(4,128)(2,1)}), bf16[16,7,4,128]{3,2,1,0:T(4,128)(2,1)S(1)}, u32[]{:S(2)}, u32[]{:S(2)}) %all-to-all-start) | async-done | bytes 114720 | tf_op jit(solution)/shard_map/all_to_all | solution.py:372
  48.2 0.7 shard_map.103
  48.9 27.9 %all_to_all.20 = bf16[32,192,128]{2,1,0:T(8,128)(2,1)S(1)} all-to-all(bf16[32,192,128]{2,1,0:T(8,128)(2,1)S(1)} %get-tuple-element.28), channel_id=1, replica_groups={{0,1,2,3,4,5,6,7,8,9,10,11,12,13,14,15,32,33,34,35,36,37,38,39,40,41,42..., dimensions={0} | all-to-all | bytes 3145728 | tf_op jit(solution)/shard_map/all_to_all | solution.py:372
  76.8 3.7 %shard_map.104 = (bf16[32,96,128]{2,1,0:T(8,128)(2,1)}, bf16[2,288,128]{2,1,0:T(8,128)(2,1)S(1)}) custom-call(bf16[2,3072,128]{2,1,0:T(8,128)(2,1)S(1)} %bitcast.10, bf16[96,3072]{1,0:T(8,128)(2,1)S(1)} %bitcast.14, bf16[96,3072]{1,0:T(8,128)(2,1)S(1)} %bitcast.16, bf16[96,3072]{1,0:T(8,128)(2,1)S(1)} %bitcast.18, bf16[96,3072]{1,0:T(8,128)(2,1)S(1)} %copy-done.4, ...), custom_call_target="tpu_custom_call" | custom-call | flops 754974720 | bytes 6291456 | tf_op jit(solution)/shard_map/pallas_call | solution.py:213
  80.5 5.3 %all-to-all-start.2 = ((bf16[32,96,128]{2,1,0:T(8,128)(2,1)}), bf16[32,96,128]{2,1,0:T(8,128)(2,1)S(1)}, u32[]{:S(2)}, u32[]{:S(2)}) async-start(bf16[32,96,128]{2,1,0:T(8,128)(2,1)} %get-tuple-element.32), calls=%async_computation.2 | async-start | bytes 1572864 | tf_op jit(solution)/shard_map/all_to_all | solution.py:372
  85.8 1.6 %shard_map.105 = bf16[3,96,3072]{2,1,0:T(8,128)(2,1)} custom-call(bf16[2,3072,128]{2,1,0:T(8,128)(2,1)S(1)} %bitcast.11, bf16[2,288,128]{2,1,0:T(8,128)(2,1)S(1)} %get-tuple-element.33.cots_ref), custom_call_target="tpu_custom_call" | custom-call | flops 226492416 | bytes 4194304 | tf_op jit(solution)/shard_map/pallas_call | solution.py:281
  87.5 1.9 %collective-permute-start.3 = (bf16[3,96,3072]{2,1,0:T(8,128)(2,1)}, bf16[3,96,3072]{2,1,0:T(8,128)(2,1)S(1)}, u32[]{:S(2)}, u32[]{:S(2)}) collective-permute-start(bf16[3,96,3072]{2,1,0:T(8,128)(2,1)} %shard_map.105), channel_id=1, source_target_pairs={{0,16},{16,0},{1,17},{17,1},{2,18},{18,2},{3,19},{19,3},{4,20},{20... | collective-permute-start | bytes 5308424 | tf_op jit(solution)/shard_map/ppermute | solution.py:288
  89.4 3.9 %collective-permute-done.3.recv_ref = bf16[3,96,3072]{2,1,0:T(8,128)(2,1)S(1)} collective-permute-done((bf16[3,96,3072]{2,1,0:T(8,128)(2,1)}, bf16[3,96,3072]{2,1,0:T(8,128)(2,1)S(1)}, u32[]{:S(2)}, u32[]{:S(2)}) %collective-permute-start.3) | collective-permute-done | bytes 1769504 | tf_op jit(solution)/shard_map/ppermute | solution.py:288
  93.3 1.8 %shard_map.106 = (bf16[96,3072]{1,0:T(8,128)(2,1)}, bf16[96,3072]{1,0:T(8,128)(2,1)}, bf16[96,3072]{1,0:T(8,128)(2,1)}) custom-call(bf16[2,3072,128]{2,1,0:T(8,128)(2,1)S(1)} %bitcast.12, bf16[2,288,128]{2,1,0:T(8,128)(2,1)S(1)} %get-tuple-element.33.cots_ref, bf16[3,96,3072]{2,1,0:T(8,128)(2,1)S(1)} %collective-permute-done.3.recv_ref), custom_call_target="tpu_custom_call" | custom-call | flops 226492416 | bytes 4194304 | tf_op jit(solution)/shard_map/pallas_call | solution.py:289
  95.0 1.8 %all-to-all-done.2.back_ref = bf16[32,96,128]{2,1,0:T(8,128)(2,1)S(1)} async-done(((bf16[32,96,128]{2,1,0:T(8,128)(2,1)}), bf16[32,96,128]{2,1,0:T(8,128)(2,1)S(1)}, u32[]{:S(2)}, u32[]{:S(2)}) %all-to-all-start.2) | async-done | bytes 786464 | tf_op jit(solution)/shard_map/all_to_all | solution.py:372
  96.8 0.5 shard_map.107
  97.3 27.1 %all_to_all.21.parts_ref = bf16[16,3,4,128]{3,2,1,0:T(4,128)(2,1)} all-to-all(bf16[16,3,4,128]{3,2,1,0:T(4,128)(2,1)S(1)} %shard_map.107), channel_id=1, replica_groups={{512,576,640,704,768,832,896,960,0,64,128,192,256,320,384,448},{544,608..., dimensions={0} | all-to-all | bytes 98304 | tf_op jit(solution)/shard_map/all_to_all | solution.py:372
  124.4 1.5 %shard_map.108 = bf16[8,192]{1,0:T(8,128)(2,1)} custom-call(bf16[16,3,4,128]{3,2,1,0:T(4,128)(2,1)} %all_to_all.21.parts_ref), custom_call_target="tpu_custom_call" | custom-call | tf_op jit(solution)/shard_map/pallas_call | solution.py:352
  (11 shorter events, 0.0 us)
Async XLA Ops:
  2.1 74.7 %copy-start = (bf16[1,96,3072]{2,1,0:T(8,128)(2,1)S(1)}, bf16[1,96,3072]{2,1,0:T(8,128)(2,1)}, u32[]{:S(2)}) copy-start(bf16[1,96,3072]{2,1,0:T(8,128)(2,1)} %param.11) | copy-start | bytes 1769476
  2.1 74.7 %copy-start.1 = (bf16[1,96,3072]{2,1,0:T(8,128)(2,1)S(1)}, bf16[1,96,3072]{2,1,0:T(8,128)(2,1)}, u32[]{:S(2)}) copy-start(bf16[1,96,3072]{2,1,0:T(8,128)(2,1)} %param.12) | copy-start | bytes 1769476
  2.1 74.7 %copy-start.2 = (bf16[1,96,3072]{2,1,0:T(8,128)(2,1)S(1)}, bf16[1,96,3072]{2,1,0:T(8,128)(2,1)}, u32[]{:S(2)}) copy-start(bf16[1,96,3072]{2,1,0:T(8,128)(2,1)} %param.13) | copy-start | bytes 1769476
  2.1 46.1 %all-to-all-start = ((bf16[16,7,4,128]{3,2,1,0:T(4,128)(2,1)}), bf16[16,7,4,128]{3,2,1,0:T(4,128)(2,1)S(1)}, u32[]{:S(2)}, u32[]{:S(2)}) async-start(bf16[16,7,4,128]{3,2,1,0:T(4,128)(2,1)} %shard_map.102), calls=%async_computation | async-start | bytes 229376 | tf_op jit(solution)/shard_map/all_to_all | solution.py:372
  32.7 6.3 %collective-permute-start = (bf16[96,3072]{1,0:T(8,128)(2,1)}, bf16[96,3072]{1,0:T(8,128)(2,1)S(1)}, u32[]{:S(2)}, u32[]{:S(2)}) collective-permute-start(bf16[96,3072]{1,0:T(8,128)(2,1)} %bitcast.13), channel_id=1, source_target_pairs={{0,16},{16,0},{1,17},{17,1},{2,18},{18,2},{3,19},{19,3},{4,20},{20... | collective-permute-start | bytes 1769480 | tf_op jit(solution)/shard_map/ppermute | solution.py:390
  34.7 5.2 %collective-permute-start.1 = (bf16[96,3072]{1,0:T(8,128)(2,1)}, bf16[96,3072]{1,0:T(8,128)(2,1)S(1)}, u32[]{:S(2)}, u32[]{:S(2)}) collective-permute-start(bf16[96,3072]{1,0:T(8,128)(2,1)} %bitcast.15), channel_id=1, source_target_pairs={{0,16},{16,0},{1,17},{17,1},{2,18},{18,2},{3,19},{19,3},{4,20},{20... | collective-permute-start | bytes 1769480 | tf_op jit(solution)/shard_map/ppermute | solution.py:390
  37.1 4.2 %collective-permute-start.2 = (bf16[96,3072]{1,0:T(8,128)(2,1)}, bf16[96,3072]{1,0:T(8,128)(2,1)}, u32[]{:S(2)}, u32[]{:S(2)}) collective-permute-start(bf16[96,3072]{1,0:T(8,128)(2,1)} %bitcast.17), channel_id=1, source_target_pairs={{0,16},{16,0},{1,17},{17,1},{2,18},{18,2},{3,19},{19,3},{4,20},{20... | collective-permute-start | bytes 1769480 | tf_op jit(solution)/shard_map/ppermute | solution.py:390
  39.0 0.8 copy-start.3
  39.8 0.8 copy-start.5
  48.2 28.6 %copy-start.4 = (bf16[96,3072]{1,0:T(8,128)(2,1)S(1)}, bf16[96,3072]{1,0:T(8,128)(2,1)}, u32[]{:S(2)}) copy-start(bf16[96,3072]{1,0:T(8,128)(2,1)} %copy-done.3) | copy-start | bytes 1769476
  48.2 28.6 %copy-start.6 = (bf16[96,3072]{1,0:T(8,128)(2,1)S(1)}, bf16[96,3072]{1,0:T(8,128)(2,1)}, u32[]{:S(2)}) copy-start(bf16[96,3072]{1,0:T(8,128)(2,1)} %copy-done.5) | copy-start | bytes 1769476
  80.5 16.2 %all-to-all-start.2 = ((bf16[32,96,128]{2,1,0:T(8,128)(2,1)}), bf16[32,96,128]{2,1,0:T(8,128)(2,1)S(1)}, u32[]{:S(2)}, u32[]{:S(2)}) async-start(bf16[32,96,128]{2,1,0:T(8,128)(2,1)} %get-tuple-element.32), calls=%async_computation.2 | async-start | bytes 1572864 | tf_op jit(solution)/shard_map/all_to_all | solution.py:372
  87.5 5.8 %collective-permute-start.3 = (bf16[3,96,3072]{2,1,0:T(8,128)(2,1)}, bf16[3,96,3072]{2,1,0:T(8,128)(2,1)S(1)}, u32[]{:S(2)}, u32[]{:S(2)}) collective-permute-start(bf16[3,96,3072]{2,1,0:T(8,128)(2,1)} %shard_map.105), channel_id=1, source_target_pairs={{0,16},{16,0},{1,17},{17,1},{2,18},{18,2},{3,19},{19,3},{4,20},{20... | collective-permute-start | bytes 5308424 | tf_op jit(solution)/shard_map/ppermute | solution.py:288
